TPU v7x, 512 devices: a whole 4x8x8 slice. The times are simulated.
512 devices in a mesh: dp: 64 (over y, x, core), proto: 8 (over z).
Axes of the slice: x: 4, y: 8, z: 8, core: 2. Of those that a mesh axis runs over, the one named last changes fastest.
Arguments:
- student_features: bfloat16 [8192, 384], P('dp'), may hold values from -160 to 160
- teacher_features: bfloat16 [8192, 384], P('dp'), may hold values from -160 to 160
- prototypes: bfloat16 [65536, 384], P(('dp', 'proto')), may hold values from -160 to 160
Outputs:
- grad_features: float32 [8192, 384], P('dp')
- grad_prototypes: float32 [65536, 384], P(('dp', 'proto'))
- losses: float32 [8192], P('dp')
All inputs are finite; a program needn't handle non-finite values.
Results may differ from a plain program's by a relative error of at most 0.0015.
Values may be sent and summed in bfloat16 or wider, within the bound.
A program may use at most 128 MiB of HBM per device.

v0:
```python
import jax
import jax.numpy as jnp
from jax import lax
from jax.sharding import PartitionSpec as P

teacher_temp = 0.07
student_temp = 0.1
norm_eps = 1e-06


def unit_rows(values):
    widened = values.astype(jnp.float32)
    inverse = lax.rsqrt(jnp.sum(widened * widened, axis=-1, keepdims=True) + norm_eps)
    return (widened * inverse, inverse)


def against_rows(features, proto_rows):
    return lax.dot_general(
        features, proto_rows, (((1,), (1,)), ((), ())), preferred_element_type=jnp.float32
    )


def scale_columns(partial_sums):
    return 1.0 / lax.psum(partial_sums, "dp")


def shards(student_features, teacher_features, prototypes):
    crop_rows = student_features.shape[0]
    crops_total = crop_rows * lax.axis_size("dp")
    proto_unit, proto_inverse = unit_rows(prototypes)
    proto_half = proto_unit.astype(jnp.bfloat16)
    student_unit, student_inverse = unit_rows(student_features)
    student_half = student_unit.astype(jnp.bfloat16)
    teacher_half = unit_rows(teacher_features)[0].astype(jnp.bfloat16)
    proto_all = lax.all_gather(proto_half, "dp", axis=0, tiled=True)
    teacher_logits = against_rows(teacher_half, proto_all)
    student_logits = against_rows(student_half, proto_all)
    teacher_expo = jnp.exp(teacher_logits * (1.0 / teacher_temp))
    column_scale = scale_columns(jnp.sum(teacher_expo, axis=0))
    for iteration in range(2):
        row_part = jnp.sum(teacher_expo * column_scale[None, :], axis=1)
        row_scale = 1.0 / lax.psum(row_part, "proto")
        column_scale = scale_columns(jnp.sum(teacher_expo * row_scale[:, None], axis=0))
    logits = student_logits * (1.0 / student_temp)
    student_expo = jnp.exp(logits)
    scaled = teacher_expo * column_scale[None, :]
    row_total, mixed_total, student_total = lax.psum(
        (jnp.sum(scaled, axis=1), jnp.sum(scaled * logits, axis=1), jnp.sum(student_expo, axis=1)),
        "proto",
    )
    row_scale = 1.0 / row_total
    target = scaled * row_scale[:, None]
    losses = jnp.log(student_total) - mixed_total * row_scale
    score_grad = ((student_expo / student_total[:, None] - target) * (1.0 / crops_total)).astype(
        jnp.bfloat16
    )
    unit_part = jnp.dot(score_grad, proto_all, preferred_element_type=jnp.float32)
    unit_grad = lax.psum(unit_part, "proto") * (1.0 / student_temp)
    grad_features = student_inverse * (
        unit_grad - student_unit * jnp.sum(student_unit * unit_grad, axis=1, keepdims=True)
    )
    column_grads = lax.all_to_all(score_grad, "dp", split_axis=1, concat_axis=0, tiled=True)
    proto_sum = lax.dot_general(
        column_grads,
        lax.all_gather(student_half, "dp", axis=0, tiled=True),
        (((0,), (0,)), ((), ())),
        preferred_element_type=jnp.float32,
    )
    proto_grad = proto_sum * (1.0 / student_temp)
    grad_prototypes = proto_inverse * (
        proto_grad - proto_unit * jnp.sum(proto_unit * proto_grad, axis=1, keepdims=True)
    )
    return (grad_features, grad_prototypes, losses)


def solution(mesh):
    in_specs = (P("dp", None), P("dp", None), P(("dp", "proto"), None))
    out_specs = (P("dp", None), P(("dp", "proto"), None), P("dp"))
    return jax.shard_map(shards, mesh=mesh, in_specs=in_specs, out_specs=out_specs, check_vma=False)
```

profile of v0, /device:TPU:1, one launch (start us, length us, event | category | flops | bytes accessed | tf_op | source)
XLA Modules:
  0.0 1101.1 jit_solution(4512645674533961838)
XLA Ops:
  8.2 1.6 fusion.3
  10.9 1.0 fusion.10
  13.0 91.2 %all-gather.3.cloned.1.call-done = bf16[8192,384]{1,0:T(8,128)(2,1)} async-done(((bf16[128,384]{1,0:T(8,128)(2,1)}), bf16[8192,384]{1,0:T(8,128)(2,1)}) %all-gather.3.cloned.1.call-update) | async-done | bytes 6291472 | tf_op jit(solution)/shard_map/all_gather | solution.py:35
  104.2 6.9 fusion.19
  111.1 242.9 %psum.64 = f32[8192]{0:T(1024)S(1)} all-reduce(f32[8192]{0:T(1024)S(1)} %get-tuple-element.11), channel_id=1, replica_groups=mesh['dp'=64,'proto'=8] {'dp'}, use_global_device_ids=true, to_apply=%region_6.0 | all-reduce | flops 8192 | bytes 65536 | tf_op jit(solution)/shard_map/psum | solution.py:24
  354.0 2.6 multiply_reduce_fusion.4
  356.6 14.5 %psum.65 = f32[128]{0:T(128)S(1)} all-reduce(f32[128]{0:T(128)S(1)} %multiply_reduce_fusion.4), channel_id=1, replica_groups=mesh['dp'=64,'proto'=8] {'proto'}, use_global_device_ids=true, to_apply=%region_8.0 | all-reduce | flops 128 | bytes 1024 | tf_op jit(solution)/shard_map/psum | solution.py:42
  371.1 2.6 multiply_reduce_fusion.3
  373.7 249.9 %psum.66 = f32[8192]{0:T(1024)S(1)} all-reduce(f32[8192]{0:T(1024)S(1)} %multiply_reduce_fusion.3), channel_id=1, replica_groups=mesh['dp'=64,'proto'=8] {'dp'}, use_global_device_ids=true, to_apply=%region_10.0 | all-reduce | flops 8192 | bytes 65536 | tf_op jit(solution)/shard_map/psum | solution.py:24
  623.6 2.6 multiply_reduce_fusion.2
  626.1 10.9 psum.67
  637.0 2.6 multiply_reduce_fusion.1
  639.7 249.9 %psum.68 = f32[8192]{0:T(1024)S(1)} all-reduce(f32[8192]{0:T(1024)S(1)} %multiply_reduce_fusion.1), channel_id=1, replica_groups=mesh['dp'=64,'proto'=8] {'dp'}, use_global_device_ids=true, to_apply=%region_14.0 | all-reduce | flops 8192 | bytes 65536 | tf_op jit(solution)/shard_map/psum | solution.py:24
  889.6 8.4 multiply_reduce_fusion
  897.9 11.9 %all-reduce = (f32[128]{0:T(128)S(1)}, f32[128]{0:T(128)S(1)}, f32[128]{0:T(128)S(1)}) all-reduce(f32[128]{0:T(128)S(1)} %get-tuple-element.4, f32[128]{0:T(128)S(1)} %get-tuple-element.5, f32[128]{0:T(128)S(1)} %get-tuple-element.3), channel_id=1, replica_groups=mesh['dp'=64,'proto'=8] {'proto'}, use_global_device_ids=true, to_apply=%region_16.0 | all-reduce | flops 384 | bytes 3072 | tf_op jit(solution)/shard_map/psum | solution.py:47
  910.3 4.5 multiply_convert_fusion
  914.9 4.7 fusion.20
  920.4 1.9 copy_bitcast_fusion
  922.3 15.0 %all-to-all-start = ((bf16[128,64,128]{2,0,1:T(8,128)(2,1)}), bf16[128,64,128]{2,0,1:T(8,128)(2,1)S(1)}, u32[]{:S(2)}, u32[]{:S(2)}) async-start(bf16[128,64,128]{2,0,1:T(8,128)(2,1)} %copy_bitcast_fusion), calls=%async_computation | async-start | bytes 4194304 | tf_op jit(solution)/shard_map/all_to_all | solution.py:62
  937.4 59.2 %all-reduce.3.cloned.1.call-done = f32[128,384]{1,0:T(8,128)} async-done(((f32[128,384]{1,0:T(8,128)}), f32[128,384]{1,0:T(8,128)}) %all-reduce.3.cloned.1.call-update) | async-done | bytes 196624 | tf_op jit(solution)/shard_map/psum | solution.py:58
  996.6 1.1 fusion.7
  997.7 1.7 fusion.9
  999.4 90.1 %all-gather.5.cloned.1.call-done = bf16[8192,384]{1,0:T(8,128)(2,1)} async-done(((bf16[128,384]{1,0:T(8,128)(2,1)}), bf16[8192,384]{1,0:T(8,128)(2,1)}) %all-gather.5.cloned.1.call-update) | async-done | bytes 6291472 | tf_op jit(solution)/shard_map/all_gather | solution.py:65
  1089.6 4.2 fusion.11
  (26 shorter events, 5.2 us)
Async XLA Ops:
  7.2 97.0 %all-gather.3.cloned.1.call-start = ((), (), s32[]{:S(2)}) async-start(), calls=%async_computation.1 | async-start | bytes 6389760 | tf_op jit(solution)/shard_map/all_gather | solution.py:35
  9.9 986.7 %all-reduce.3.cloned.1.call-start = ((), (), s32[]{:S(2)}) async-start(), calls=%async_computation.2 | async-start | bytes 393216 | tf_op jit(solution)/shard_map/psum | solution.py:58
  12.9 876.6 %copy-start.2 = (bf16[128,384]{1,0:T(8,128)(2,1)}, bf16[128,384]{1,0:T(8,128)(2,1)S(1)}, u32[]{:S(2)}) copy-start(bf16[128,384]{1,0:T(8,128)(2,1)S(1)} %fusion.6) | copy-start | bytes 294916
  919.6 170.0 %all-gather.5.cloned.1.call-start = ((), (), s32[]{:S(2)}) async-start(), calls=%async_computation.3 | async-start | bytes 6389760 | tf_op jit(solution)/shard_map/all_gather | solution.py:65
  920.4 76.2 %copy-start.1 = (bf16[128,384]{1,0:T(8,128)(2,1)S(1)}, bf16[128,384]{1,0:T(8,128)(2,1)}, u32[]{:S(2)}) copy-start(bf16[128,384]{1,0:T(8,128)(2,1)} %param.3) | copy-start | bytes 294916
  920.4 169.2 %copy-start = (bf16[128,384]{1,0:T(8,128)(2,1)S(1)}, bf16[128,384]{1,0:T(8,128)(2,1)}, u32[]{:S(2)}) copy-start(bf16[128,384]{1,0:T(8,128)(2,1)} %param.5) | copy-start | bytes 294916
  922.3 167.3 %all-to-all-start = ((bf16[128,64,128]{2,0,1:T(8,128)(2,1)}), bf16[128,64,128]{2,0,1:T(8,128)(2,1)S(1)}, u32[]{:S(2)}, u32[]{:S(2)}) async-start(bf16[128,64,128]{2,0,1:T(8,128)(2,1)} %copy_bitcast_fusion), calls=%async_computation | async-start | bytes 4194304 | tf_op jit(solution)/shard_map/all_to_all | solution.py:62
Sparse Core Ops, SparseCore 0:
  11.9 92.1 all-gather.2
  919.8 76.8 all-reduce.2
  1000.5 89.0 all-gather.4
where the time goes:
time: 1100 us
  blocking collectives  780 us (71%)
  waiting for transfers between devices  241 us (22%)
  other arithmetic  24.7 us (2%)
  matrix products  24.2 us (2%)
  starting transfers between devices  15.1 us (1%)
  between operations  13.9 us (1%)
    psum x3, blocking collectives, scale_columns(): return 1.0 / lax.psum(partial_sums, 'dp')  743 us
    all_gather x1, waiting for transfers between devices, shards(): proto_all = lax.all_gather(proto_half, 'dp', axis=0, tiled=True)  91.2 us
    all_gather x1, waiting for transfers between devices, shards(): lax.all_gather(student_half, 'dp', axis=0, tiled=True)  90.1 us
    psum x1, waiting for transfers between devices, shards(): unit_grad = lax.psum(unit_part, 'proto') * (1.0 / student_temp)  59.2 us
    psum x2, blocking collectives, shards(): row_scale = 1.0 / lax.psum(row_part, 'proto')  25.4 us
  transfers between devices with their start and end apart: 4, of which 3 were waited for; matrix products, arithmetic and copies ran while one was open for 1% of the time, Pallas kernels for 0%

commit v1 on v0

v1 whole, which is shorter than its diff:
```python
import jax
import jax.numpy as jnp
from jax import lax
from jax.experimental import pallas as pl
from jax.experimental.pallas import tpu as pltpu
from jax.sharding import PartitionSpec as P

NY, NX, NC, NZ = 8, 4, 2, 8
NP = NX * NC
B = 128
K = 384
R = NY * B
C = NP * B
PIECE = B // NZ
CROPS = NY * NX * NC * B
TEACHER = 1.0 / 0.07
STUDENT = 1.0 / 0.1
EPS = 1e-06
MESH = pl.DeviceIdType.MESH
F32, BF16 = jnp.float32, jnp.bfloat16


def unit_rows(values):
    widened = values.astype(F32)
    inverse = lax.rsqrt(jnp.sum(widened * widened, axis=-1, keepdims=True) + EPS)
    return widened * inverse, inverse


def against_rows(a, b):
    return lax.dot_general(a, b, (((1,), (1,)), ((), ())), preferred_element_type=F32)


def project(unit, grad, inverse):
    return inverse * (grad - unit * jnp.sum(unit * grad, axis=1, keepdims=True))


def kernel(
    s_ref, t_ref, p_ref, gf_ref, gp_ref, loss_ref,
    t_all, s_all, s_turned, p_all, e_ref, l_ref, x_ref, g_ref, su_ref, pu_ref, sinv_ref, pinv_ref,
    colx, rowy, rowz, lasty, lastz, col_now, row_now, last_now,
    u_ref, near, zfar, w_ref, yfar, b_ref, zn, gfb, v_ref, vsib, vx,
    ts, tr, ss, sr, ps, pr, xs, xr, ys, yr, zs, zr, us, ur, vs, vr,
):
    dp, z = lax.axis_index("dp"), lax.axis_index("proto")
    core = lax.rem(dp, NC)
    x = lax.rem(lax.div(dp, NC), NX)
    y = lax.div(dp, NC * NX)
    own = core * NX + x

    def at_y(other):
        return ((other * NX + x) * NC + core, z)

    def at_z(other):
        return (dp, other)

    def at_p(other):
        return ((y * NX + lax.rem(other, NX)) * NC + lax.div(other, NX), z)

    def ring(value, size):
        return lax.rem(value + size, size)

    def copy(src, dst, send, recv, device):
        return pltpu.make_async_remote_copy(
            src_ref=src, dst_ref=dst, send_sem=send, recv_sem=recv, device_id=device, device_id_type=MESH
        )

    def each(first, last, body):
        def step(i, carry):
            body(i)
            return carry

        lax.fori_loop(first, last, step, 0)

    barrier = pltpu.get_barrier_semaphore()

    def greet(q):
        for device in (at_y(ring(y + q, NY)), at_p(ring(own + q, NP)), at_z(ring(z + q, NZ))):
            pl.semaphore_signal(barrier, inc=1, device_id=device, device_id_type=MESH)

    each(1, 8, greet)

    t_all[0] = unit_rows(t_ref[...])[0].astype(BF16)
    p_unit, p_inverse = unit_rows(p_ref[...])
    p_all[own] = p_unit.astype(BF16)
    pu_ref[...] = p_unit
    pinv_ref[...] = jnp.broadcast_to(p_inverse, (B, 128))
    s_unit, s_inverse = unit_rows(s_ref[...])
    s_all[0] = s_unit.astype(BF16)
    su_ref[...] = s_unit
    sinv_ref[...] = jnp.broadcast_to(s_inverse, (B, 128))
    pl.semaphore_wait(barrier, 21)

    def rows(who):
        return pl.ds(pl.multiple_of(who * PIECE, PIECE), PIECE)

    def far_copy(ref, send, recv, d):
        part = (d, rows(z))
        return copy(ref.at[0, rows(z)], ref.at[part], send.at[d], recv.at[d], at_y(ring(y - d, NY)))

    def near_copy(ref, send, recv, d):
        return copy(ref.at[0], ref.at[d], send.at[d], recv.at[d], at_y(ring(y - d, NY)))

    def pass_copy(ref, send, recv, j, source, target):
        part = ref.at[pl.ds(3, 3), rows(source)]
        return copy(part, part, send.at[8 + j], recv.at[8 + j], at_z(target))

    def near_d(i):
        return ring((lax.div(i, 2) + 1) * (1 - 2 * lax.rem(i, 2)), NY)

    def gather_start(ref, send, recv):
        each(3, 6, lambda d: far_copy(ref, send, recv, d).start())
        each(0, 4, lambda i: near_copy(ref, send, recv, near_d(i)).start())

    def gather_pass(ref, send, recv):
        each(3, 6, lambda d: far_copy(ref, send, recv, d).wait_recv())
        each(1, 8, lambda j: pass_copy(ref, send, recv, j, z, ring(z + j, NZ)).start())

    def gather_far(ref, send, recv):
        each(1, 8, lambda j: pass_copy(ref, send, recv, j, ring(z - j, NZ), ring(z + j, NZ)).wait_recv())

    def gather_sent(ref, send, recv):
        each(3, 6, lambda d: far_copy(ref, send, recv, d).wait_send())
        each(0, 4, lambda i: near_copy(ref, send, recv, near_d(i)).wait_send())
        each(1, 8, lambda j: pass_copy(ref, send, recv, j, z, ring(z + j, NZ)).wait_send())

    def x_copy(j, source, target):
        part = p_all.at[core * NX + source]
        return copy(part, part, ps.at[j], pr.at[j], at_p(core * NX + target))

    def sib_copy(j, who):
        part = p_all.at[who * NX + ring(x - j, NX)]
        return copy(part, part, ps.at[4 + j], pr.at[4 + j], at_p((1 - core) * NX + x))

    each(1, 4, lambda j: x_copy(j, x, ring(x + j, NX)).start())
    gather_start(t_all, ts, tr)
    sib_copy(0, core).start()
    gather_pass(t_all, ts, tr)

    def hand_over(j):
        x_copy(j, ring(x - j, NX), ring(x + j, NX)).wait_recv()
        sib_copy(j, core).start()

    each(1, 4, hand_over)
    each(0, 4, lambda j: sib_copy(j, 1 - core).wait_recv())

    def crop_rows(d):
        return pl.ds(pl.multiple_of(d * B, B), B)

    def proto_pair(n):
        return p_all[2 * n : 2 * n + 2].reshape(2 * B, K)

    col_now[...] = jnp.zeros((8, C), F32)

    def teacher_block(d):
        block = t_all[d]
        for n in range(C // 256):
            lanes = slice(n * 256, (n + 1) * 256)
            expo = jnp.exp(against_rows(block, proto_pair(n)) * TEACHER)
            e_ref[crop_rows(d), lanes] = expo
            col_now[:, lanes] += jnp.sum(expo.reshape(B // 8, 8, 256), axis=0)

    teacher_block(0)

    def near_teacher(i):
        d = near_d(i)
        near_copy(t_all, ts, tr, d).wait_recv()
        teacher_block(d)

    each(0, 4, near_teacher)
    gather_start(s_all, ss, sr)
    gather_far(t_all, ts, tr)
    each(3, 6, teacher_block)

    def swap_start(buf, send, recv, mine, at):
        part = buf.at[mine]
        each(1, 8, lambda q: copy(part, part, send.at[q], recv.at[mine], at(ring(mine + q, 8))).start())

    def swap_wait(buf, send, recv, mine, at):
        def one(q):
            source = ring(mine + q, 8)
            part = buf.at[source]
            copy(part, part, send.at[q], recv.at[source], at(source)).wait_recv()

        each(1, 8, one)
        total = buf[0]
        for i in range(1, 8):
            total = total + buf[i]
        return total

    def swap_sent(buf, send, recv, mine, at):
        part = buf.at[mine]
        each(1, 8, lambda q: copy(part, part, send.at[q], recv.at[mine], at(ring(mine + q, 8))).wait_send())

    def col_swap(it):
        return colx.at[it], xs.at[it], xr.at[it], own, at_p

    def y_swap(it):
        return (rowy.at[it] if it < 2 else lasty), ys.at[it], yr.at[it], y, at_y

    def z_swap(it):
        return (rowz.at[it] if it < 2 else lastz), zs.at[it], zr.at[it], z, at_z

    def lane_rows(tile):
        return jnp.sum(tile.T, axis=0, keepdims=True)

    def down(vector):
        return jnp.broadcast_to(vector, (B, B)).T

    def lane_tile(k):
        return slice(k * B, (k + 1) * B)

    def student_block(d):
        block = s_all[d]
        total = jnp.zeros((B, B), F32)
        for n in range(C // 256):
            lanes = slice(n * 256, (n + 1) * 256)
            logits = against_rows(block, proto_pair(n)) * STUDENT
            expo = jnp.exp(logits)
            l_ref[crop_rows(d), lanes] = logits
            x_ref[crop_rows(d), lanes] = expo
            total = total + expo[:, :B] + expo[:, B:]
        lasty[y, pl.ds(16 + ring(y + d, NY), 1), :] = lane_rows(total)
        s_turned[:, crop_rows(d)] = block.T

    def near_student(i):
        d = near_d(i)
        near_copy(s_all, ss, sr, d).wait_recv()
        student_block(d)

    def weigh_rows(it):
        scale = col_now[:, :B]

        def block(d):
            total = jnp.zeros((B, B), F32)
            for k in range(NP):
                total = total + e_ref[crop_rows(d), lane_tile(k)] * scale[k : k + 1, :]
            rowy[it, y, pl.ds(ring(y + d, NY), 1), :] = lane_rows(total)

        each(0, NY, block)

    def weigh_columns(it):
        def block(d, totals):
            scale = down(row_now[pl.ds(ring(y + d, NY), 1), :])
            return tuple(
                totals[k]
                + jnp.sum((e_ref[crop_rows(d), lane_tile(k)] * scale).reshape(B // 8, 8, B), axis=0)
                for k in range(NP)
            )

        totals = lax.fori_loop(0, NY, block, (jnp.zeros((8, B), F32),) * NP)
        for k in range(NP):
            colx[it, own, k : k + 1, :] = jnp.sum(totals[k], axis=0, keepdims=True)

    for k in range(NP):
        colx[0, own, k : k + 1, :] = jnp.sum(col_now[:, lane_tile(k)], axis=0, keepdims=True)
    swap_start(*col_swap(0))
    gather_pass(s_all, ss, sr)
    student_block(0)
    col_now[:, :B] = 1.0 / swap_wait(*col_swap(0))
    for it in range(2):
        weigh_rows(it)
        swap_start(*y_swap(it))
        if it == 0:
            near_student(0)
        else:
            student_block(3)
        rowz[it, z] = swap_wait(*y_swap(it))
        swap_start(*z_swap(it))
        if it == 0:
            near_student(1)
            near_student(2)
        else:
            student_block(4)
        row_now[...] = 1.0 / swap_wait(*z_swap(it))
        weigh_columns(it + 1)
        swap_start(*col_swap(it + 1))
        if it == 0:
            near_student(3)
            gather_far(s_all, ss, sr)
        else:
            student_block(5)
        col_now[:, :B] = 1.0 / swap_wait(*col_swap(it + 1))

    def last_rows(d):
        scale = col_now[:, :B]
        total, mixed = jnp.zeros((B, B), F32), jnp.zeros((B, B), F32)
        for k in range(NP):
            scaled = e_ref[crop_rows(d), lane_tile(k)] * scale[k : k + 1, :]
            total = total + scaled
            mixed = mixed + scaled * l_ref[crop_rows(d), lane_tile(k)]
        lasty[y, pl.ds(ring(y + d, NY), 1), :] = lane_rows(total)
        lasty[y, pl.ds(8 + ring(y + d, NY), 1), :] = lane_rows(mixed)

    each(0, NY, last_rows)
    swap_start(*y_swap(2))
    lastz[z] = swap_wait(*y_swap(2))
    swap_start(*z_swap(2))
    last_now[...] = swap_wait(*z_swap(2))
    mine = pl.ds(y, 1)
    row_total, mixed_total, student_total = last_now[0:8], last_now[8:16], last_now[16:24]
    row_now[...] = jnp.log(student_total) - mixed_total / row_total
    loss_ref[...] = row_now[mine, :]
    last_now[0:8] = 1.0 / row_total
    last_now[16:24] = 1.0 / student_total

    def grad_block(d):
        b = ring(y + d, NY)
        scale = col_now[:, :B]
        row_scale, student_scale = down(last_now[pl.ds(b, 1), :]), down(last_now[pl.ds(16 + b, 1), :])
        for k in range(NP):
            target = e_ref[crop_rows(d), lane_tile(k)] * scale[k : k + 1, :] * row_scale
            g_ref[crop_rows(d), lane_tile(k)] = (
                x_ref[crop_rows(d), lane_tile(k)] * student_scale - target
            ).astype(BF16)
        u_ref[d] = jnp.dot(g_ref[crop_rows(d), :], p_all[...].reshape(C, K), preferred_element_type=F32)

    def u_far(j, source, target):
        return copy(
            u_ref.at[pl.ds(3, 3), rows(target)], zfar.at[source], us.at[j], ur.at[j], at_z(target)
        )

    def u_near(d):
        return copy(u_ref.at[d], near.at[d], us.at[8 + d], ur.at[8 + d], at_y(ring(y + d, NY)))

    def u_sum(k):
        return copy(w_ref.at[k], yfar.at[k], us.at[16 + k], ur.at[16 + k], at_y(ring(y + 3 + k, NY)))

    def u_piece(j, source, target):
        return copy(b_ref.at[rows(target)], zn.at[source], us.at[24 + j], ur.at[24 + j], at_z(target))

    def u_all(j, source, target):
        part = gfb.at[rows(source)]
        return copy(part, part, us.at[32 + j], ur.at[32 + j], at_z(target))

    def z_start(make):
        each(1, NZ, lambda j: make(j, z, ring(z + j, NZ)).start())

    def z_wait(make):
        each(1, NZ, lambda j: make(j, ring(z - j, NZ), ring(z + j, NZ)).wait_recv())

    def z_sent(make):
        each(1, NZ, lambda j: make(j, z, ring(z + j, NZ)).wait_send())

    each(3, 6, grad_block)
    z_start(u_far)

    def near_grad(i):
        d = near_d(i)
        grad_block(d)
        u_near(d).start()

    each(0, 4, near_grad)
    grad_block(0)

    def proto_grad(half):
        def pair(n):
            first = pl.multiple_of((half * 2 + n) * 256, 256)
            both = jnp.dot(s_turned[...], g_ref[:, pl.ds(first, 256)], preferred_element_type=F32)
            v_ref[half * NX + 2 * n] = both[:, :B]
            v_ref[half * NX + 2 * n + 1] = both[:, B:]

        each(0, 2, pair)

    def v_sib(who):
        return copy(v_ref.at[pl.ds(who * NX, NX)], vsib, vs.at[0], vr.at[0], at_p((1 - core) * NX + x))

    def v_x(j, source, target):
        return copy(
            v_ref.at[core * NX + target], vx.at[source], vs.at[j], vr.at[j], at_p(core * NX + target)
        )

    proto_grad(1 - core)
    v_sib(1 - core).start()
    proto_grad(core)

    z_wait(u_far)
    zfar[z] = u_ref[pl.ds(3, 3), rows(z)]
    total = zfar[0]
    for i in range(1, NZ):
        total = total + zfar[i]
    w_ref[...] = total
    each(0, 3, lambda k: u_sum(k).start())

    v_sib(1 - core).wait_recv()

    def add_sibling(i):
        v_ref[core * NX + i] += vsib[i]

    each(0, NX, add_sibling)
    each(1, NX, lambda j: v_x(j, x, ring(x + j, NX)).start())

    each(0, 4, lambda i: u_near(near_d(i)).wait_recv())
    b_ref[...] = u_ref[0] + near[1] + near[2] + near[6] + near[7]
    z_start(u_piece)

    each(1, NX, lambda j: v_x(j, ring(x - j, NX), ring(x + j, NX)).wait_recv())
    vx[x] = v_ref[own]
    proto_sum = (vx[0] + vx[1] + vx[2] + vx[3]).T * (STUDENT / CROPS)
    gp_ref[...] = project(pu_ref[...], proto_sum, pinv_ref[:, 0:1])

    z_wait(u_piece)
    each(0, 3, lambda k: u_sum(k).wait_recv())
    zn[z] = b_ref[rows(z)]
    total = yfar[0] + yfar[1] + yfar[2]
    for i in range(NZ):
        total = total + zn[i]
    gfb[rows(z)] = project(su_ref[rows(z)], total * (STUDENT / CROPS), sinv_ref[rows(z), 0:1])
    z_start(u_all)
    z_wait(u_all)
    gf_ref[...] = gfb[...]

    each(1, 4, lambda j: x_copy(j, x, ring(x + j, NX)).wait_send())
    each(0, 4, lambda j: sib_copy(j, core).wait_send())
    gather_sent(t_all, ts, tr)
    gather_sent(s_all, ss, sr)
    for it in range(3):
        swap_sent(*col_swap(it))
        swap_sent(*y_swap(it))
        swap_sent(*z_swap(it))
    z_sent(u_far)
    each(0, 4, lambda i: u_near(near_d(i)).wait_send())
    each(0, 3, lambda k: u_sum(k).wait_send())
    z_sent(u_piece)
    z_sent(u_all)
    v_sib(1 - core).wait_send()
    each(1, NX, lambda j: v_x(j, x, ring(x + j, NX)).wait_send())


def shards(student_features, teacher_features, prototypes):
    vmem = pl.BlockSpec(memory_space=pltpu.VMEM)
    dma = pltpu.SemaphoreType.DMA
    grad_features, grad_prototypes, losses = pl.pallas_call(
        kernel,
        out_shape=(
            jax.ShapeDtypeStruct((B, K), F32),
            jax.ShapeDtypeStruct((B, K), F32),
            jax.ShapeDtypeStruct((1, B), F32),
        ),
        in_specs=[vmem] * 3,
        out_specs=(vmem,) * 3,
        scratch_shapes=[
            pltpu.VMEM((NY, B, K), BF16),
            pltpu.VMEM((NY, B, K), BF16),
            pltpu.VMEM((K, R), BF16),
            pltpu.VMEM((NP, B, K), BF16),
            pltpu.VMEM((R, C), F32),
            pltpu.VMEM((R, C), F32),
            pltpu.VMEM((R, C), F32),
            pltpu.VMEM((R, C), BF16),
            pltpu.VMEM((B, K), F32),
            pltpu.VMEM((B, K), F32),
            pltpu.VMEM((B, 128), F32),
            pltpu.VMEM((B, 128), F32),
            pltpu.VMEM((3, 8, 8, 128), F32),
            pltpu.VMEM((2, 8, 8, 128), F32),
            pltpu.VMEM((2, 8, 8, 128), F32),
            pltpu.VMEM((8, 24, 128), F32),
            pltpu.VMEM((8, 24, 128), F32),
            pltpu.VMEM((8, C), F32),
            pltpu.VMEM((8, 128), F32),
            pltpu.VMEM((24, 128), F32),
            pltpu.VMEM((NY, B, K), F32),
            pltpu.VMEM((NY, B, K), F32),
            pltpu.VMEM((NZ, 3, PIECE, K), F32),
            pltpu.VMEM((3, PIECE, K), F32),
            pltpu.VMEM((3, PIECE, K), F32),
            pltpu.VMEM((B, K), F32),
            pltpu.VMEM((NZ, PIECE, K), F32),
            pltpu.VMEM((B, K), F32),
            pltpu.VMEM((NP, K, B), F32),
            pltpu.VMEM((NX, K, B), F32),
            pltpu.VMEM((NX, K, B), F32),
            dma((16,)), dma((16,)),
            dma((16,)), dma((16,)),
            dma((8,)), dma((8,)),
            dma((3, 8)), dma((3, 8)),
            dma((3, 8)), dma((3, 8)),
            dma((3, 8)), dma((3, 8)),
            dma((40,)), dma((40,)),
            dma((4,)), dma((4,)),
        ],
        compiler_params=pltpu.CompilerParams(
            collective_id=0, has_side_effects=True, vmem_limit_bytes=50 * 1024 * 1024
        ),
        name="dino_head",
    )(student_features, teacher_features, prototypes)
    return grad_features, grad_prototypes, losses.reshape(B)


def solution(mesh):
    in_specs = (P("dp", None), P("dp", None), P(("dp", "proto"), None))
    out_specs = (P("dp", None), P(("dp", "proto"), None), P("dp"))
    return jax.shard_map(shards, mesh=mesh, in_specs=in_specs, out_specs=out_specs, check_vma=False)
```

time: 1100 us -> 115 us (0.10)
  blocking collectives: 780 us -> 0 us
  waiting for transfers between devices: 241 us -> 0 us
  Pallas kernels: 0 us -> 109 us
  other arithmetic: 24.7 us -> 0 us
  matrix products: 24.2 us -> 0 us
  starting transfers between devices: 15.1 us -> 0 us
  between operations: 13.9 us -> 0.65 us
    psum x6 -> x0, blocking collectives: 780 us -> none  [the longest x3 743 us: scale_columns(): return 1.0 / lax.psum(partial_sums, 'dp')]
    all_gather x2 -> x0, waiting for transfers between devices: 181 us -> none  [the longest x1 91.2 us: shards(): proto_all = lax.all_gather(proto_half, 'dp', axis=0, tiled=True)]
    pallas_call x0 -> x1, Pallas kernels: none -> 109 us  [shards(): pl.pallas_call(kernel, out_shape=(jax.ShapeDtypeStruct((B, K), F32), jax....]
    psum x1 -> x0, waiting for transfers between devices: 59.2 us -> none  [shards(): unit_grad = lax.psum(unit_part, 'proto') * (1.0 / student_temp)]
    dot_general x4 -> x0, matrix products: 24.2 us -> none  [the longest x2 15.3 us: against_rows(): lax.dot_general(features, proto_rows, (((1,), (1,)), ((), ())), preferred...]
    all_to_all x1 -> x0, starting transfers between devices: 15 us -> none  [shards(): lax.all_to_all(score_grad, 'dp', split_axis=1, concat_axis=0, tiled=True)]
    reduce_sum x8 -> x0, other arithmetic: 14.4 us -> none  [the longest x2 5.21 us: shards(): jnp.sum(teacher_expo * row_scale[:, None], axis=0)]
  transfers between devices with their start and end apart: 4 -> 0, of which waited for: 3 -> 0; matrix products, arithmetic and copies ran while one was open for 1% -> 0% of each run, Pallas kernels for 0% -> 0%
where the time goes in v1:
time: 115 us; the launch traced here: 114 us
  Pallas kernels  109 us (95%)
  local copies, waits for them, and re-layouts  4.54 us (4%)
    pallas_call x1, Pallas kernels, shards(): pl.pallas_call(kernel, out_shape=(jax.ShapeDtypeStruct((B, K), F32), jax....  109 us
    unnamed x9, local copies, waits for them, and re-layouts  4.54 us

profile of v1, /device:TPU:1, one launch (start us, length us, event | category | flops | bytes accessed | tf_op | source)
XLA Modules:
  0.0 113.7 jit_solution(14334776962688223821)
XLA Ops:
  0.6 0.0 copy-start
  0.6 0.9 copy-done
  1.5 0.0 copy-start.1
  1.5 0.9 copy-done.1
  2.4 0.0 copy-start.2
  2.4 0.9 copy-done.2
  3.3 108.6 %dino_head.1 = (f32[128,384]{1,0:T(8,128)S(1)}, f32[128,384]{1,0:T(8,128)S(1)}, f32[1,128]{1,0:T(1,128)S(1)}) custom-call(bf16[128,384]{1,0:T(8,128)(2,1)S(1)} %copy-done, bf16[128,384]{1,0:T(8,128)(2,1)S(1)} %copy-done.1, bf16[128,384]{1,0:T(8,128)(2,1)S(1)} %copy-done.2), custom_call_target="tpu_custom_call" | custom-call | tf_op jit(solution)/shard_map/dino_head/pallas_call | solution.py:432
  111.9 0.7 copy.9
  112.6 0.7 copy.10
  113.2 0.5 copy.11
Async XLA Ops:
  0.6 0.9 copy-start
  1.5 0.9 copy-start.1
  2.4 0.9 copy-start.2

commit v2 on v1

v2 whole, which is shorter than its diff:
```python
import jax
import jax.numpy as jnp
from jax import lax
from jax.experimental import pallas as pl
from jax.experimental.pallas import tpu as pltpu
from jax.sharding import PartitionSpec as P

NY, NX, NC, NZ = 8, 4, 2, 8
NP = NX * NC
B = 128
K = 384
R = NY * B
C = NP * B
PIECE = B // NZ
CROPS = NY * NX * NC * B
TEACHER = 1.0 / 0.07
STUDENT = 1.0 / 0.1
EPS = 1e-06
MESH = pl.DeviceIdType.MESH
F32, BF16 = jnp.float32, jnp.bfloat16


def unit_rows(values):
    widened = values.astype(F32)
    inverse = lax.rsqrt(jnp.sum(widened * widened, axis=-1, keepdims=True) + EPS)
    return widened * inverse, inverse


def against_rows(a, b):
    return lax.dot_general(a, b, (((1,), (1,)), ((), ())), preferred_element_type=F32)


def project(unit, grad, inverse):
    return inverse * (grad - unit * jnp.sum(unit * grad, axis=1, keepdims=True))


def kernel(
    s_hbm, t_hbm, p_hbm, gf_ref, gp_ref, loss_ref,
    s_ref, t_ref, p_ref,
    t_all, s_all, s_turned, p_all, e_ref, l_ref, x_ref, g_ref, su_ref, pu_ref, sinv_ref, pinv_ref,
    colx, rowy, rowz, lasty, lastz, col_now, row_now, last_now,
    lo_ref, down_ref, us_ref, s_near_in, s_zfar, s_w, s_yfar, s_b, s_zn,
    ut_ref, t_near_in, t_zfar, t_w, t_yfar, t_b, t_zn, gfb, v_ref, vsib, vx,
    ins, ts, tr, ss, sr, ps, pr, xs, xr, ys, yr, zs, zr, uss, usr, uts, utr, gs, gr, vs, vr,
):
    dp, z = lax.axis_index("dp"), lax.axis_index("proto")
    core = lax.rem(dp, NC)
    x = lax.rem(lax.div(dp, NC), NX)
    y = lax.div(dp, NC * NX)
    own = core * NX + x

    def at_y(other):
        return ((other * NX + x) * NC + core, z)

    def at_z(other):
        return (dp, other)

    def at_p(other):
        return ((y * NX + lax.rem(other, NX)) * NC + lax.div(other, NX), z)

    def ring(value, size):
        return lax.rem(value + size, size)

    def copy(src, dst, send, recv, device):
        return pltpu.make_async_remote_copy(
            src_ref=src, dst_ref=dst, send_sem=send, recv_sem=recv, device_id=device, device_id_type=MESH
        )

    def each(first, last, body):
        def step(i, carry):
            body(i)
            return carry

        lax.fori_loop(first, last, step, 0)

    loads = [
        pltpu.make_async_copy(far, here, ins.at[i])
        for i, (far, here) in enumerate(((t_hbm, t_ref), (p_hbm, p_ref), (s_hbm, s_ref)))
    ]
    for load in loads:
        load.start()

    barrier = pltpu.get_barrier_semaphore()

    def greet(q):
        for device in (at_y(ring(y + q, NY)), at_p(ring(own + q, NP)), at_z(ring(z + q, NZ))):
            pl.semaphore_signal(barrier, inc=1, device_id=device, device_id_type=MESH)

    each(1, 8, greet)

    for load in loads:
        load.wait()
    t_all[0] = unit_rows(t_ref[...])[0].astype(BF16)
    p_unit, p_inverse = unit_rows(p_ref[...])
    p_all[own] = p_unit.astype(BF16)
    pu_ref[...] = p_unit
    pinv_ref[...] = jnp.broadcast_to(p_inverse, (B, 128))
    s_unit, s_inverse = unit_rows(s_ref[...])
    s_all[0] = s_unit.astype(BF16)
    su_ref[...] = s_unit
    sinv_ref[...] = jnp.broadcast_to(s_inverse, (B, 128))
    pl.semaphore_wait(barrier, 21)

    log = []

    class Copies:
        def __init__(self, first, last, out, into):
            self.first, self.last, self.out, self.into = first, last, out, into
            self.left = set(range(first, last))

        def start(self):
            log.append(self)
            each(self.first, self.last, lambda i: self.out(i).start())

        def start_one(self, i):
            if self not in log:
                log.append(self)
            self.out(i).start()

        def recv(self):
            self.left.clear()
            each(self.first, self.last, lambda i: self.into(i).wait_recv())

        def recv_one(self, i):
            if isinstance(i, int):
                self.left.discard(i)
            else:
                self.left.clear()
            self.into(i).wait_recv()

        def sent(self):
            each(self.first, self.last, lambda i: self.out(i).wait_send())

    def rows(who):
        return pl.ds(pl.multiple_of(who * PIECE, PIECE), PIECE)

    def crop_rows(d):
        return pl.ds(pl.multiple_of(d * B, B), B)

    def near_d(i):
        return ring((lax.div(i, 2) + 1) * (1 - 2 * lax.rem(i, 2)), NY)

    def over_z(make):
        return Copies(1, NZ, lambda j: make(j, z, ring(z + j, NZ)), lambda j: make(j, ring(z - j, NZ), ring(z + j, NZ)))

    def gather(ref, send, recv):
        def far_copy(d):
            return copy(
                ref.at[0, rows(z)], ref.at[d, rows(z)], send.at[d], recv.at[d], at_y(ring(y - d, NY))
            )

        def near_copy(i):
            d = near_d(i)
            return copy(ref.at[0], ref.at[d], send.at[d], recv.at[d], at_y(ring(y - d, NY)))

        def pass_copy(j, source, target):
            part = ref.at[pl.ds(3, 3), rows(source)]
            return copy(part, part, send.at[8 + j], recv.at[8 + j], at_z(target))

        return Copies(3, 6, far_copy, far_copy), Copies(0, 4, near_copy, near_copy), over_z(pass_copy)

    t_far, t_near, t_pass = gather(t_all, ts, tr)
    s_far, s_near, s_pass = gather(s_all, ss, sr)

    def x_copy(j, source, target):
        part = p_all.at[core * NX + source]
        return copy(part, part, ps.at[j], pr.at[j], at_p(core * NX + target))

    def over_x(make):
        return Copies(1, NX, lambda j: make(j, x, ring(x + j, NX)), lambda j: make(j, ring(x - j, NX), ring(x + j, NX)))

    def sib_copy(j, who):
        part = p_all.at[who * NX + ring(x - j, NX)]
        return copy(part, part, ps.at[4 + j], pr.at[4 + j], at_p((1 - core) * NX + x))

    p_x = over_x(x_copy)
    p_own = Copies(0, 1, lambda j: sib_copy(j, core), lambda j: sib_copy(j, 1 - core))
    p_passed = Copies(1, NX, lambda j: sib_copy(j, core), lambda j: sib_copy(j, 1 - core))

    p_x.start()
    t_far.start()
    t_near.start()
    p_own.start()
    s_far.start()
    t_far.recv()
    t_pass.start()
    p_x.recv()
    p_passed.start()
    s_far.recv()
    p_own.recv()
    p_passed.recv()
    s_pass.start()
    s_near.start()

    def proto_pair(n):
        return p_all[2 * n : 2 * n + 2].reshape(2 * B, K)

    col_now[...] = jnp.zeros((8, C), F32)

    def teacher_block(d):
        block = t_all[d]
        for n in range(C // 256):
            lanes = slice(n * 256, (n + 1) * 256)
            expo = jnp.exp(against_rows(block, proto_pair(n)) * TEACHER)
            e_ref[crop_rows(d), lanes] = expo
            col_now[:, lanes] += jnp.sum(expo.reshape(B // 8, 8, 256), axis=0)

    teacher_block(0)

    def near_teacher(i):
        t_near.recv_one(i)
        teacher_block(near_d(i))

    each(0, 4, near_teacher)
    t_pass.recv()
    each(3, 6, teacher_block)

    class Swap(Copies):
        def __init__(self, buf, send, recv, mine, at):
            def out(q):
                return copy(buf.at[mine], buf.at[mine], send.at[q], recv.at[mine], at(ring(mine + q, 8)))

            def into(q):
                source = ring(mine + q, 8)
                return copy(buf.at[source], buf.at[source], send.at[q], recv.at[source], at(source))

            super().__init__(1, 8, out, into)
            self.buf = buf

        def start(self):
            log.append(self)
            for q in (4, 3, 5, 2, 6, 1, 7):
                self.out(q).start()

        def total(self):
            self.left.clear()
            for q in (1, 7, 2, 6, 3, 5, 4):
                self.into(q).wait_recv()
            total = self.buf[0]
            for i in range(1, 8):
                total = total + self.buf[i]
            return total

    col_swap = [Swap(colx.at[it], xs.at[it], xr.at[it], own, at_p) for it in range(3)]
    y_swap = [Swap(rowy.at[it], ys.at[it], yr.at[it], y, at_y) for it in range(2)]
    z_swap = [Swap(rowz.at[it], zs.at[it], zr.at[it], z, at_z) for it in range(2)]
    last_y = Swap(lasty, ys.at[2], yr.at[2], y, at_y)
    last_z = Swap(lastz, zs.at[2], zr.at[2], z, at_z)

    def lane_rows(tile):
        return jnp.sum(tile.T, axis=0, keepdims=True)

    def down(vector):
        return jnp.broadcast_to(vector, (B, B)).T

    def lane_tile(k):
        return slice(k * B, (k + 1) * B)

    def split(d, lanes, values):
        high = values.astype(BF16)
        g_ref[crop_rows(d), lanes] = high
        lo_ref[:, lanes] = (values - high.astype(F32)).astype(BF16)

    def split_times_protos(d):
        protos = p_all[...].reshape(C, K)
        return jnp.dot(g_ref[crop_rows(d), :], protos, preferred_element_type=F32) + jnp.dot(
            lo_ref[...], protos, preferred_element_type=F32
        )

    class Reduce:
        def __init__(self, u, near, zfar, w, yfar, b, zn, send, recv):
            self.bufs = u, near, zfar, w, yfar, b, zn

            def far_copy(j, source, target):
                part = u.at[pl.ds(3, 3), rows(target)]
                return copy(part, zfar.at[source], send.at[j], recv.at[j], at_z(target))

            def near_copy(i):
                d = near_d(i)
                return copy(u.at[d], near.at[i], send.at[8 + i], recv.at[8 + i], at_y(ring(y + d, NY)))

            def sum_copy(k):
                to = at_y(ring(y + 3 + k, NY))
                return copy(w.at[k], yfar.at[k], send.at[12 + k], recv.at[12 + k], to)

            def piece_copy(j, source, target):
                return copy(b.at[rows(target)], zn.at[source], send.at[16 + j], recv.at[16 + j], at_z(target))

            self.far, self.piece = over_z(far_copy), over_z(piece_copy)
            self.near, self.sum = Copies(0, 4, near_copy, near_copy), Copies(0, 3, sum_copy, sum_copy)

        def far_sums(self):
            u, _, zfar, w, _, _, _ = self.bufs
            self.far.recv()
            zfar[z] = u[pl.ds(3, 3), rows(z)]
            total = zfar[0]
            for i in range(1, NZ):
                total = total + zfar[i]
            w[...] = total
            self.sum.start()

        def near_sums(self):
            u, near, _, _, _, b, _ = self.bufs
            self.near.recv()
            b[...] = u[0] + near[0] + near[1] + near[2] + near[3]
            self.piece.start()

        def result(self):
            _, _, _, _, yfar, b, zn = self.bufs
            self.piece.recv()
            self.sum.recv()
            zn[z] = b[rows(z)]
            total = yfar[0] + yfar[1] + yfar[2]
            for i in range(NZ):
                total = total + zn[i]
            return total

    s_reduce = Reduce(us_ref, s_near_in, s_zfar, s_w, s_yfar, s_b, s_zn, uss, usr)
    t_reduce = Reduce(ut_ref, t_near_in, t_zfar, t_w, t_yfar, t_b, t_zn, uts, utr)
    us_near = s_reduce.near

    def student_block(d):
        block = s_all[d]
        total = jnp.zeros((B, B), F32)
        for n in range(C // 256):
            lanes = slice(n * 256, (n + 1) * 256)
            logits = against_rows(block, proto_pair(n)) * STUDENT
            expo = jnp.exp(logits)
            l_ref[crop_rows(d), lanes] = logits
            x_ref[crop_rows(d), lanes] = expo
            split(d, lanes, expo)
            total = total + expo[:, :B] + expo[:, B:]
        lasty[y, pl.ds(16 + ring(y + d, NY), 1), :] = lane_rows(total)
        s_turned[:, crop_rows(d)] = block.T
        us_ref[d] = split_times_protos(d)

    def near_student(i):
        s_near.recv_one(i)
        student_block(near_d(i))
        us_near.start_one(i)

    def weigh_rows(it):
        scale = col_now[:, :B]

        def block(d):
            total = jnp.zeros((B, B), F32)
            for k in range(NP):
                total = total + e_ref[crop_rows(d), lane_tile(k)] * scale[k : k + 1, :]
            rowy[it, y, pl.ds(ring(y + d, NY), 1), :] = lane_rows(total)

        each(0, NY, block)

    def weigh_columns(it):
        def block(d, totals):
            scale = down(row_now[pl.ds(ring(y + d, NY), 1), :])
            return tuple(
                totals[k]
                + jnp.sum((e_ref[crop_rows(d), lane_tile(k)] * scale).reshape(B // 8, 8, B), axis=0)
                for k in range(NP)
            )

        totals = lax.fori_loop(0, NY, block, (jnp.zeros((8, B), F32),) * NP)
        for k in range(NP):
            colx[it, own, k : k + 1, :] = jnp.sum(totals[k], axis=0, keepdims=True)

    for k in range(NP):
        colx[0, own, k : k + 1, :] = jnp.sum(col_now[:, lane_tile(k)], axis=0, keepdims=True)
    col_swap[0].start()
    student_block(0)
    col_now[:, :B] = 1.0 / col_swap[0].total()
    for it in range(2):
        weigh_rows(it)
        y_swap[it].start()
        if it == 0:
            near_student(0)
            near_student(1)
        else:
            student_block(5)
            s_reduce.far.start()
        rowz[it, z] = y_swap[it].total()
        z_swap[it].start()
        if it == 0:
            near_student(2)
            near_student(3)
        row_now[...] = 1.0 / z_swap[it].total()
        weigh_columns(it + 1)
        col_swap[it + 1].start()
        if it == 0:
            s_pass.recv()
            student_block(3)
            student_block(4)
        col_now[:, :B] = 1.0 / col_swap[it + 1].total()

    def last_rows(d):
        scale = col_now[:, :B]
        total, mixed = jnp.zeros((B, B), F32), jnp.zeros((B, B), F32)
        for k in range(NP):
            scaled = e_ref[crop_rows(d), lane_tile(k)] * scale[k : k + 1, :]
            total = total + scaled
            mixed = mixed + scaled * l_ref[crop_rows(d), lane_tile(k)]
        lasty[y, pl.ds(ring(y + d, NY), 1), :] = lane_rows(total)
        lasty[y, pl.ds(8 + ring(y + d, NY), 1), :] = lane_rows(mixed)

    each(0, NY, last_rows)
    last_y.start()

    def teacher_grad(d):
        scale = col_now[:, :B]
        for k in range(NP):
            split(d, lane_tile(k), e_ref[crop_rows(d), lane_tile(k)] * scale[k : k + 1, :])
        ut_ref[d] = split_times_protos(d)

    each(3, 6, teacher_grad)
    t_reduce.far.start()

    def near_grad(i):
        teacher_grad(near_d(i))
        t_reduce.near.out(i).start()

    log.append(t_reduce.near)
    each(0, 4, near_grad)
    lastz[z] = last_y.total()
    last_z.start()
    teacher_grad(0)
    s_reduce.near_sums()
    s_reduce.far_sums()
    last_now[...] = last_z.total()
    row_total, mixed_total, student_total = last_now[0:8], last_now[8:16], last_now[16:24]
    row_now[...] = jnp.log(student_total) - mixed_total / row_total
    loss_ref[...] = row_now[pl.ds(y, 1), :]
    last_now[0:8] = 1.0 / row_total
    last_now[16:24] = 1.0 / student_total
    down_ref[0] = down(last_now[pl.ds(y, 1), :])
    down_ref[1] = down(last_now[pl.ds(16 + y, 1), :])

    def grad_block(d):
        b = ring(y + d, NY)
        scale = col_now[:, :B]
        row_scale, student_scale = down(last_now[pl.ds(b, 1), :]), down(last_now[pl.ds(16 + b, 1), :])
        for k in range(NP):
            target = e_ref[crop_rows(d), lane_tile(k)] * scale[k : k + 1, :] * row_scale
            g_ref[crop_rows(d), lane_tile(k)] = (
                x_ref[crop_rows(d), lane_tile(k)] * student_scale - target
            ).astype(BF16)

    each(0, NY, grad_block)

    def proto_grad(half):
        def pair(n):
            first = pl.multiple_of((half * 2 + n) * 256, 256)
            both = jnp.dot(s_turned[...], g_ref[:, pl.ds(first, 256)], preferred_element_type=F32)
            v_ref[half * NX + 2 * n] = both[:, :B]
            v_ref[half * NX + 2 * n + 1] = both[:, B:]

        each(0, 2, pair)

    def v_sib_copy(who):
        return copy(v_ref.at[pl.ds(who * NX, NX)], vsib, vs.at[0], vr.at[0], at_p((1 - core) * NX + x))

    def v_x_copy(j, source, target):
        return copy(
            v_ref.at[core * NX + target], vx.at[source], vs.at[j], vr.at[j], at_p(core * NX + target)
        )

    v_sib = Copies(0, 1, lambda i: v_sib_copy(1 - core), lambda i: v_sib_copy(1 - core))
    v_x = over_x(v_x_copy)

    proto_grad(1 - core)
    v_sib.start()
    proto_grad(core)

    v_sib.recv()

    def add_sibling(i):
        v_ref[core * NX + i] += vsib[i]

    each(0, NX, add_sibling)
    v_x.start()
    t_reduce.near_sums()
    t_reduce.far_sums()

    v_x.recv()
    vx[x] = v_ref[own]
    proto_sum = (vx[0] + vx[1] + vx[2] + vx[3]).T * (STUDENT / CROPS)
    gp_ref[...] = project(pu_ref[...], proto_sum, pinv_ref[:, 0:1])
    student_part = s_reduce.result() * down_ref[1, rows(z), 0:1]
    teacher_part = t_reduce.result() * down_ref[0, rows(z), 0:1]
    unit_grad = (student_part - teacher_part) * (STUDENT / CROPS)
    gfb[rows(z)] = project(su_ref[rows(z)], unit_grad, sinv_ref[rows(z), 0:1])

    def all_copy(j, source, target):
        part = gfb.at[rows(source)]
        return copy(part, part, gs.at[j], gr.at[j], at_z(target))

    every = over_z(all_copy)
    every.start()
    every.recv()
    gf_ref[...] = gfb[...]

    for group in log:
        group.sent()


def reduce_shapes():
    return [
        pltpu.VMEM((NY, B, K), F32),
        pltpu.VMEM((4, B, K), F32),
        pltpu.VMEM((NZ, 3, PIECE, K), F32),
        pltpu.VMEM((3, PIECE, K), F32),
        pltpu.VMEM((3, PIECE, K), F32),
        pltpu.VMEM((B, K), F32),
        pltpu.VMEM((NZ, PIECE, K), F32),
    ]


def shards(student_features, teacher_features, prototypes):
    vmem = pl.BlockSpec(memory_space=pltpu.VMEM)
    dma = pltpu.SemaphoreType.DMA
    grad_features, grad_prototypes, losses = pl.pallas_call(
        kernel,
        out_shape=(
            jax.ShapeDtypeStruct((B, K), F32),
            jax.ShapeDtypeStruct((B, K), F32),
            jax.ShapeDtypeStruct((1, B), F32),
        ),
        in_specs=[pl.BlockSpec(memory_space=pltpu.MemorySpace.HBM)] * 3,
        out_specs=(vmem,) * 3,
        scratch_shapes=[
            pltpu.VMEM((B, K), BF16), pltpu.VMEM((B, K), BF16), pltpu.VMEM((B, K), BF16),
            pltpu.VMEM((NY, B, K), BF16),
            pltpu.VMEM((NY, B, K), BF16),
            pltpu.VMEM((K, R), BF16),
            pltpu.VMEM((NP, B, K), BF16),
            pltpu.VMEM((R, C), F32),
            pltpu.VMEM((R, C), F32),
            pltpu.VMEM((R, C), F32),
            pltpu.VMEM((R, C), BF16),
            pltpu.VMEM((B, K), F32),
            pltpu.VMEM((B, K), F32),
            pltpu.VMEM((B, 128), F32),
            pltpu.VMEM((B, 128), F32),
            pltpu.VMEM((3, 8, 8, 128), F32),
            pltpu.VMEM((2, 8, 8, 128), F32),
            pltpu.VMEM((2, 8, 8, 128), F32),
            pltpu.VMEM((8, 24, 128), F32),
            pltpu.VMEM((8, 24, 128), F32),
            pltpu.VMEM((8, C), F32),
            pltpu.VMEM((8, 128), F32),
            pltpu.VMEM((24, 128), F32),
            pltpu.VMEM((B, C), BF16),
            pltpu.VMEM((2, B, 128), F32),
            *reduce_shapes(),
            *reduce_shapes(),
            pltpu.VMEM((B, K), F32),
            pltpu.VMEM((NP, K, B), F32),
            pltpu.VMEM((NX, K, B), F32),
            pltpu.VMEM((NX, K, B), F32),
            dma((3,)),
            dma((16,)), dma((16,)),
            dma((16,)), dma((16,)),
            dma((8,)), dma((8,)),
            dma((3, 8)), dma((3, 8)),
            dma((3, 8)), dma((3, 8)),
            dma((3, 8)), dma((3, 8)),
            dma((24,)), dma((24,)),
            dma((24,)), dma((24,)),
            dma((8,)), dma((8,)),
            dma((4,)), dma((4,)),
        ],
        compiler_params=pltpu.CompilerParams(
            collective_id=0, has_side_effects=True, vmem_limit_bytes=60 * 1024 * 1024
        ),
        name="dino_head",
    )(student_features, teacher_features, prototypes)
    return grad_features, grad_prototypes, losses.reshape(B)


def solution(mesh):
    in_specs = (P("dp", None), P("dp", None), P(("dp", "proto"), None))
    out_specs = (P("dp", None), P(("dp", "proto"), None), P("dp"))
    return jax.shard_map(shards, mesh=mesh, in_specs=in_specs, out_specs=out_specs, check_vma=False)
```

time: 115 us -> 125 us (1.087)
  Pallas kernels: 109 us -> 121 us
  local copies, waits for them, and re-layouts: 4.54 us -> 2.85 us
    pallas_call x1, Pallas kernels: 109 us -> 121 us  [shards(): pl.pallas_call(kernel, out_shape=(jax.ShapeDtypeStruct((B, K), F32), jax....]
    unnamed x9 -> x7, local copies, waits for them, and re-layouts: 4.54 us -> 2.85 us
where the time goes in v2:
time: 125 us; the launch traced here: 124 us
  Pallas kernels  121 us (97%)
  local copies, waits for them, and re-layouts  2.85 us (2%)
    pallas_call x1, Pallas kernels, shards(): pl.pallas_call(kernel, out_shape=(jax.ShapeDtypeStruct((B, K), F32), jax....  121 us
    unnamed x7, local copies, waits for them, and re-layouts  2.85 us

profile of v2, /device:TPU:1, one launch (start us, length us, event | category | flops | bytes accessed | tf_op | source)
XLA Modules:
  0.0 124.5 jit_solution(1144201456331880257)
XLA Ops:
  0.6 121.0 %dino_head.1 = (f32[128,384]{1,0:T(8,128)}, f32[128,384]{1,0:T(8,128)}, f32[1,128]{1,0:T(1,128)}) custom-call(bf16[128,384]{1,0:T(8,128)(2,1)} %s_hbm.1, bf16[128,384]{1,0:T(8,128)(2,1)} %t_hbm.1, bf16[128,384]{1,0:T(8,128)(2,1)} %p_hbm.1), custom_call_target="tpu_custom_call" | custom-call | tf_op jit(solution)/shard_map/dino_head/pallas_call | solution.py:519
  121.6 0.0 copy-start
  121.6 1.7 %copy.9 = f32[128,384]{1,0:T(8,128)} copy(f32[128,384]{1,0:T(8,128)} %get-tuple-element.12) | data formatting | bytes 393216
  123.3 0.0 copy-done
  123.3 0.0 copy-start.1
  123.3 0.7 copy.10
  124.0 0.0 copy-done.1
  124.0 0.5 copy.11
Async XLA Ops:
  121.6 1.7 %copy-start = (f32[128,384]{1,0:T(8,128)S(1)}, f32[128,384]{1,0:T(8,128)}, u32[]{:S(2)}) copy-start(f32[128,384]{1,0:T(8,128)} %get-tuple-element.13) | copy-start | bytes 589828
  123.3 0.7 copy-start.1

commit v3 on v2

--- a/solution.py
+++ b/solution.py
@@ -39,8 +39,8 @@
     s_ref, t_ref, p_ref,
     t_all, s_all, s_turned, p_all, e_ref, l_ref, x_ref, g_ref, su_ref, pu_ref, sinv_ref, pinv_ref,
     colx, rowy, rowz, lasty, lastz, col_now, row_now, last_now,
-    lo_ref, down_ref, us_ref, s_near_in, s_zfar, s_w, s_yfar, s_b, s_zn,
-    ut_ref, t_near_in, t_zfar, t_w, t_yfar, t_b, t_zn, gfb, v_ref, vsib, vx,
+    down_ref, us_ref, us_own, s_near_in, s_zfar, s_w, s_yfar, s_b, s_zn,
+    ut_ref, ut_own, t_near_in, t_zfar, t_w, t_yfar, t_b, t_zn, gfb, v_ref, vsib, vx,
     ins, ts, tr, ss, sr, ps, pr, xs, xr, ys, yr, zs, zr, uss, usr, uts, utr, gs, gr, vs, vr,
 ):
     dp, z = lax.axis_index("dp"), lax.axis_index("proto")
@@ -112,11 +112,6 @@
             log.append(self)
             each(self.first, self.last, lambda i: self.out(i).start())
 
-        def start_one(self, i):
-            if self not in log:
-                log.append(self)
-            self.out(i).start()
-
         def recv(self):
             self.left.clear()
             each(self.first, self.last, lambda i: self.into(i).wait_recv())
@@ -189,7 +184,6 @@
     s_far.recv()
     p_own.recv()
     p_passed.recv()
-    s_pass.start()
     s_near.start()
 
     def proto_pair(n):
@@ -213,6 +207,7 @@
 
     each(0, 4, near_teacher)
     t_pass.recv()
+    s_pass.start()
     each(3, 6, teacher_block)
 
     class Swap(Copies):
@@ -256,20 +251,12 @@
     def lane_tile(k):
         return slice(k * B, (k + 1) * B)
 
-    def split(d, lanes, values):
-        high = values.astype(BF16)
-        g_ref[crop_rows(d), lanes] = high
-        lo_ref[:, lanes] = (values - high.astype(F32)).astype(BF16)
-
-    def split_times_protos(d):
-        protos = p_all[...].reshape(C, K)
-        return jnp.dot(g_ref[crop_rows(d), :], protos, preferred_element_type=F32) + jnp.dot(
-            lo_ref[...], protos, preferred_element_type=F32
-        )
+    def times_protos(d):
+        return jnp.dot(g_ref[crop_rows(d), :], p_all[...].reshape(C, K), preferred_element_type=F32)
 
     class Reduce:
-        def __init__(self, u, near, zfar, w, yfar, b, zn, send, recv):
-            self.bufs = u, near, zfar, w, yfar, b, zn
+        def __init__(self, u, u_own, near, zfar, w, yfar, b, zn, send, recv):
+            self.bufs = u, u_own, near, zfar, w, yfar, b, zn
 
             def far_copy(j, source, target):
                 part = u.at[pl.ds(3, 3), rows(target)]
@@ -289,24 +276,31 @@
             self.far, self.piece = over_z(far_copy), over_z(piece_copy)
             self.near, self.sum = Copies(0, 4, near_copy, near_copy), Copies(0, 3, sum_copy, sum_copy)
 
+        def put(self, d, block):
+            u, u_own = self.bufs[:2]
+            if isinstance(d, int) and d == 0:
+                u_own[...] = block
+            else:
+                u[d] = block.astype(BF16)
+
         def far_sums(self):
-            u, _, zfar, w, _, _, _ = self.bufs
+            u, _, _, zfar, w, _, _, _ = self.bufs
             self.far.recv()
             zfar[z] = u[pl.ds(3, 3), rows(z)]
-            total = zfar[0]
+            total = zfar[0].astype(F32)
             for i in range(1, NZ):
-                total = total + zfar[i]
+                total = total + zfar[i].astype(F32)
             w[...] = total
             self.sum.start()
 
         def near_sums(self):
-            u, near, _, _, _, b, _ = self.bufs
+            _, u_own, near, _, _, _, b, _ = self.bufs
             self.near.recv()
-            b[...] = u[0] + near[0] + near[1] + near[2] + near[3]
+            b[...] = u_own[...] + sum(near[i].astype(F32) for i in range(4))
             self.piece.start()
 
         def result(self):
-            _, _, _, _, yfar, b, zn = self.bufs
+            _, _, _, _, _, yfar, b, zn = self.bufs
             self.piece.recv()
             self.sum.recv()
             zn[z] = b[rows(z)]
@@ -315,9 +309,8 @@
                 total = total + zn[i]
             return total
 
-    s_reduce = Reduce(us_ref, s_near_in, s_zfar, s_w, s_yfar, s_b, s_zn, uss, usr)
-    t_reduce = Reduce(ut_ref, t_near_in, t_zfar, t_w, t_yfar, t_b, t_zn, uts, utr)
-    us_near = s_reduce.near
+    s_reduce = Reduce(us_ref, us_own, s_near_in, s_zfar, s_w, s_yfar, s_b, s_zn, uss, usr)
+    t_reduce = Reduce(ut_ref, ut_own, t_near_in, t_zfar, t_w, t_yfar, t_b, t_zn, uts, utr)
 
     def student_block(d):
         block = s_all[d]
@@ -328,16 +321,15 @@
             expo = jnp.exp(logits)
             l_ref[crop_rows(d), lanes] = logits
             x_ref[crop_rows(d), lanes] = expo
-            split(d, lanes, expo)
+            g_ref[crop_rows(d), lanes] = expo.astype(BF16)
             total = total + expo[:, :B] + expo[:, B:]
         lasty[y, pl.ds(16 + ring(y + d, NY), 1), :] = lane_rows(total)
         s_turned[:, crop_rows(d)] = block.T
-        us_ref[d] = split_times_protos(d)
+        s_reduce.put(d, times_protos(d))
 
     def near_student(i):
         s_near.recv_one(i)
         student_block(near_d(i))
-        us_near.start_one(i)
 
     def weigh_rows(it):
         scale = col_now[:, :B]
@@ -374,21 +366,22 @@
         if it == 0:
             near_student(0)
             near_student(1)
-        else:
-            student_block(5)
-            s_reduce.far.start()
+            near_student(2)
+            near_student(3)
         rowz[it, z] = y_swap[it].total()
         z_swap[it].start()
         if it == 0:
-            near_student(2)
-            near_student(3)
+            s_pass.recv()
+            each(3, 6, student_block)
         row_now[...] = 1.0 / z_swap[it].total()
+        if it == 0:
+            s_reduce.far.start()
+            s_reduce.near.start()
+        else:
+            s_reduce.far_sums()
+            s_reduce.near_sums()
         weigh_columns(it + 1)
         col_swap[it + 1].start()
-        if it == 0:
-            s_pass.recv()
-            student_block(3)
-            student_block(4)
         col_now[:, :B] = 1.0 / col_swap[it + 1].total()
 
     def last_rows(d):
@@ -407,8 +400,10 @@
     def teacher_grad(d):
         scale = col_now[:, :B]
         for k in range(NP):
-            split(d, lane_tile(k), e_ref[crop_rows(d), lane_tile(k)] * scale[k : k + 1, :])
-        ut_ref[d] = split_times_protos(d)
+            g_ref[crop_rows(d), lane_tile(k)] = (
+                e_ref[crop_rows(d), lane_tile(k)] * scale[k : k + 1, :]
+            ).astype(BF16)
+        t_reduce.put(d, times_protos(d))
 
     each(3, 6, teacher_grad)
     t_reduce.far.start()
@@ -422,8 +417,6 @@
     lastz[z] = last_y.total()
     last_z.start()
     teacher_grad(0)
-    s_reduce.near_sums()
-    s_reduce.far_sums()
     last_now[...] = last_z.total()
     row_total, mixed_total, student_total = last_now[0:8], last_now[8:16], last_now[16:24]
     row_now[...] = jnp.log(student_total) - mixed_total / row_total
@@ -503,9 +496,10 @@
 
 def reduce_shapes():
     return [
-        pltpu.VMEM((NY, B, K), F32),
-        pltpu.VMEM((4, B, K), F32),
-        pltpu.VMEM((NZ, 3, PIECE, K), F32),
+        pltpu.VMEM((NY, B, K), BF16),
+        pltpu.VMEM((B, K), F32),
+        pltpu.VMEM((4, B, K), BF16),
+        pltpu.VMEM((NZ, 3, PIECE, K), BF16),
         pltpu.VMEM((3, PIECE, K), F32),
         pltpu.VMEM((3, PIECE, K), F32),
         pltpu.VMEM((B, K), F32),
@@ -547,7 +541,6 @@
             pltpu.VMEM((8, C), F32),
             pltpu.VMEM((8, 128), F32),
             pltpu.VMEM((24, 128), F32),
-            pltpu.VMEM((B, C), BF16),
             pltpu.VMEM((2, B, 128), F32),
             *reduce_shapes(),
             *reduce_shapes(),

time: 125 us -> 109 us (0.87)
  Pallas kernels: 121 us -> 105 us
    pallas_call x1, Pallas kernels: 121 us -> 105 us  [shards(): pl.pallas_call(kernel, out_shape=(jax.ShapeDtypeStruct((B, K), F32), jax....]
where the time goes in v3:
time: 109 us
  Pallas kernels  105 us (96%)
  local copies, waits for them, and re-layouts  2.85 us (3%)
    pallas_call x1, Pallas kernels, shards(): pl.pallas_call(kernel, out_shape=(jax.ShapeDtypeStruct((B, K), F32), jax....  105 us
    unnamed x7, local copies, waits for them, and re-layouts  2.85 us

profile of v3, /device:TPU:1, one launch (start us, length us, event | category | flops | bytes accessed | tf_op | source)
XLA Modules:
  0.0 108.6 jit_solution(2686158103859830974)
XLA Ops:
  0.6 105.1 %dino_head.1 = (f32[128,384]{1,0:T(8,128)}, f32[128,384]{1,0:T(8,128)}, f32[1,128]{1,0:T(1,128)}) custom-call(bf16[128,384]{1,0:T(8,128)(2,1)} %s_hbm.1, bf16[128,384]{1,0:T(8,128)(2,1)} %t_hbm.1, bf16[128,384]{1,0:T(8,128)(2,1)} %p_hbm.1), custom_call_target="tpu_custom_call" | custom-call | tf_op jit(solution)/shard_map/dino_head/pallas_call | solution.py:513
  105.7 0.0 copy-start
  105.7 1.7 %copy.9 = f32[128,384]{1,0:T(8,128)} copy(f32[128,384]{1,0:T(8,128)} %get-tuple-element.12) | data formatting | bytes 393216
  107.4 0.0 copy-done
  107.4 0.0 copy-start.1
  107.4 0.7 copy.10
  108.1 0.0 copy-done.1
  108.1 0.5 copy.11
Async XLA Ops:
  105.7 1.7 %copy-start = (f32[128,384]{1,0:T(8,128)S(1)}, f32[128,384]{1,0:T(8,128)}, u32[]{:S(2)}) copy-start(f32[128,384]{1,0:T(8,128)} %get-tuple-element.13) | copy-start | bytes 589828
  107.4 0.7 copy-start.1

commit v4 on v3

--- a/solution.py
+++ b/solution.py
@@ -38,7 +38,7 @@
     s_hbm, t_hbm, p_hbm, gf_ref, gp_ref, loss_ref,
     s_ref, t_ref, p_ref,
     t_all, s_all, s_turned, p_all, e_ref, l_ref, x_ref, g_ref, su_ref, pu_ref, sinv_ref, pinv_ref,
-    colx, rowy, rowz, lasty, lastz, col_now, row_now, last_now,
+    colx, rowy, rowz, col_now, row_now, last_now,
     down_ref, us_ref, us_own, s_near_in, s_zfar, s_w, s_yfar, s_b, s_zn,
     ut_ref, ut_own, t_near_in, t_zfar, t_w, t_yfar, t_b, t_zn, gfb, v_ref, vsib, vx,
     ins, ts, tr, ss, sr, ps, pr, xs, xr, ys, yr, zs, zr, uss, usr, uts, utr, gs, gr, vs, vr,
@@ -66,12 +66,12 @@
             src_ref=src, dst_ref=dst, send_sem=send, recv_sem=recv, device_id=device, device_id_type=MESH
         )
 
-    def each(first, last, body):
+    def each(first, last, body, unroll=1):
         def step(i, carry):
             body(i)
             return carry
 
-        lax.fori_loop(first, last, step, 0)
+        lax.fori_loop(first, last, step, 0, unroll=unroll)
 
     loads = [
         pltpu.make_async_copy(far, here, ins.at[i])
@@ -112,6 +112,11 @@
             log.append(self)
             each(self.first, self.last, lambda i: self.out(i).start())
 
+        def start_all(self):
+            log.append(self)
+            for i in range(self.first, self.last):
+                self.out(i).start()
+
         def recv(self):
             self.left.clear()
             each(self.first, self.last, lambda i: self.into(i).wait_recv())
@@ -124,7 +129,8 @@
             self.into(i).wait_recv()
 
         def sent(self):
-            each(self.first, self.last, lambda i: self.out(i).wait_send())
+            for i in range(self.first, self.last):
+                self.out(i).wait_send()
 
     def rows(who):
         return pl.ds(pl.multiple_of(who * PIECE, PIECE), PIECE)
@@ -154,8 +160,28 @@
 
         return Copies(3, 6, far_copy, far_copy), Copies(0, 4, near_copy, near_copy), over_z(pass_copy)
 
-    t_far, t_near, t_pass = gather(t_all, ts, tr)
     s_far, s_near, s_pass = gather(s_all, ss, sr)
+
+    def step(k):
+        def hand_on(i):
+            side, half = i % 2, pl.ds(i // 2 * (B // 2), B // 2)
+            there, here = (k, k - 1) if side == 0 else (NY - k, (NY + 1 - k) % NY)
+            to = at_y(ring(y - 1, NY)) if side == 0 else at_y(ring(y + 1, NY))
+            index = 4 * (k - 1) + i
+            return copy(t_all.at[here, half], t_all.at[there, half], ts.at[index], tr.at[index], to)
+
+        return Copies(0, 4, hand_on, hand_on)
+
+    def t_piece_copy(i):
+        part = (4, rows(z))
+        return copy(t_all.at[0, rows(z)], t_all.at[part], ts.at[12], tr.at[12], at_y(ring(y + 4, NY)))
+
+    def t_pass_copy(j, source, target):
+        part = t_all.at[4, rows(source)]
+        return copy(part, part, ts.at[12 + j], tr.at[12 + j], at_z(target))
+
+    t_steps = [step(k) for k in (1, 2, 3)]
+    t_piece, t_pass = Copies(0, 1, t_piece_copy, t_piece_copy), over_z(t_pass_copy)
 
     def x_copy(j, source, target):
         part = p_all.at[core * NX + source]
@@ -172,19 +198,24 @@
     p_own = Copies(0, 1, lambda j: sib_copy(j, core), lambda j: sib_copy(j, 1 - core))
     p_passed = Copies(1, NX, lambda j: sib_copy(j, core), lambda j: sib_copy(j, 1 - core))
 
+    t_piece.start()
     p_x.start()
-    t_far.start()
-    t_near.start()
+    t_steps[0].start_all()
     p_own.start()
+    for now, later in zip(t_steps, t_steps[1:]):
+        log.append(later)
+        for i in range(4):
+            now.recv_one(i)
+            later.out(i).start()
+        if later is t_steps[1]:
+            t_piece.recv()
+            t_pass.start()
     s_far.start()
-    t_far.recv()
-    t_pass.start()
     p_x.recv()
     p_passed.start()
-    s_far.recv()
     p_own.recv()
+    s_near.start()
     p_passed.recv()
-    s_near.start()
 
     def proto_pair(n):
         return p_all[2 * n : 2 * n + 2].reshape(2 * B, K)
@@ -199,16 +230,16 @@
             e_ref[crop_rows(d), lanes] = expo
             col_now[:, lanes] += jnp.sum(expo.reshape(B // 8, 8, 256), axis=0)
 
-    teacher_block(0)
-
-    def near_teacher(i):
-        t_near.recv_one(i)
-        teacher_block(near_d(i))
-
-    each(0, 4, near_teacher)
+    for d in (0, 1, 7, 2, 6):
+        teacher_block(d)
+    for i in range(4):
+        t_steps[2].recv_one(i)
+    for d in (3, 5):
+        teacher_block(d)
     t_pass.recv()
+    s_far.recv()
     s_pass.start()
-    each(3, 6, teacher_block)
+    teacher_block(4)
 
     class Swap(Copies):
         def __init__(self, buf, send, recv, mine, at):
@@ -239,8 +270,12 @@
     col_swap = [Swap(colx.at[it], xs.at[it], xr.at[it], own, at_p) for it in range(3)]
     y_swap = [Swap(rowy.at[it], ys.at[it], yr.at[it], y, at_y) for it in range(2)]
     z_swap = [Swap(rowz.at[it], zs.at[it], zr.at[it], z, at_z) for it in range(2)]
-    last_y = Swap(lasty, ys.at[2], yr.at[2], y, at_y)
-    last_z = Swap(lastz, zs.at[2], zr.at[2], z, at_z)
+    last_y = Swap(rowy.at[2], ys.at[2], yr.at[2], y, at_y)
+    last_z = Swap(rowz.at[2], zs.at[2], zr.at[2], z, at_z)
+    student_y = Swap(rowy.at[3], ys.at[3], yr.at[3], y, at_y)
+    student_z = Swap(rowz.at[3], zs.at[3], zr.at[3], z, at_z)
+    mixed_y = Swap(rowy.at[4], ys.at[4], yr.at[4], y, at_y)
+    mixed_z = Swap(rowz.at[4], zs.at[4], zr.at[4], z, at_z)
 
     def lane_rows(tile):
         return jnp.sum(tile.T, axis=0, keepdims=True)
@@ -323,7 +358,7 @@
             x_ref[crop_rows(d), lanes] = expo
             g_ref[crop_rows(d), lanes] = expo.astype(BF16)
             total = total + expo[:, :B] + expo[:, B:]
-        lasty[y, pl.ds(16 + ring(y + d, NY), 1), :] = lane_rows(total)
+        rowy[3, y, pl.ds(ring(y + d, NY), 1), :] = lane_rows(total)
         s_turned[:, crop_rows(d)] = block.T
         s_reduce.put(d, times_protos(d))
 
@@ -340,7 +375,7 @@
                 total = total + e_ref[crop_rows(d), lane_tile(k)] * scale[k : k + 1, :]
             rowy[it, y, pl.ds(ring(y + d, NY), 1), :] = lane_rows(total)
 
-        each(0, NY, block)
+        each(0, NY, block, 8)
 
     def weigh_columns(it):
         def block(d, totals):
@@ -351,7 +386,7 @@
                 for k in range(NP)
             )
 
-        totals = lax.fori_loop(0, NY, block, (jnp.zeros((8, B), F32),) * NP)
+        totals = lax.fori_loop(0, NY, block, (jnp.zeros((8, B), F32),) * NP, unroll=8)
         for k in range(NP):
             colx[it, own, k : k + 1, :] = jnp.sum(totals[k], axis=0, keepdims=True)
 
@@ -372,12 +407,15 @@
         z_swap[it].start()
         if it == 0:
             s_pass.recv()
-            each(3, 6, student_block)
+            each(3, 6, student_block, 3)
         row_now[...] = 1.0 / z_swap[it].total()
         if it == 0:
+            student_y.start()
             s_reduce.far.start()
             s_reduce.near.start()
         else:
+            rowz[3, z] = student_y.total()
+            student_z.start()
             s_reduce.far_sums()
             s_reduce.near_sums()
         weigh_columns(it + 1)
@@ -386,15 +424,20 @@
 
     def last_rows(d):
         scale = col_now[:, :B]
-        total, mixed = jnp.zeros((B, B), F32), jnp.zeros((B, B), F32)
+        total = jnp.zeros((B, B), F32)
+        for k in range(NP):
+            total = total + e_ref[crop_rows(d), lane_tile(k)] * scale[k : k + 1, :]
+        rowy[2, y, pl.ds(ring(y + d, NY), 1), :] = lane_rows(total)
+
+    def mixed_rows(d):
+        scale = col_now[:, :B]
+        mixed = jnp.zeros((B, B), F32)
         for k in range(NP):
             scaled = e_ref[crop_rows(d), lane_tile(k)] * scale[k : k + 1, :]
-            total = total + scaled
             mixed = mixed + scaled * l_ref[crop_rows(d), lane_tile(k)]
-        lasty[y, pl.ds(ring(y + d, NY), 1), :] = lane_rows(total)
-        lasty[y, pl.ds(8 + ring(y + d, NY), 1), :] = lane_rows(mixed)
-
-    each(0, NY, last_rows)
+        rowy[4, y, pl.ds(ring(y + d, NY), 1), :] = lane_rows(mixed)
+
+    each(0, NY, last_rows, 8)
     last_y.start()
 
     def teacher_grad(d):
@@ -405,7 +448,7 @@
             ).astype(BF16)
         t_reduce.put(d, times_protos(d))
 
-    each(3, 6, teacher_grad)
+    each(3, 6, teacher_grad, 3)
     t_reduce.far.start()
 
     def near_grad(i):
@@ -413,30 +456,30 @@
         t_reduce.near.out(i).start()
 
     log.append(t_reduce.near)
-    each(0, 4, near_grad)
-    lastz[z] = last_y.total()
+    each(0, 4, near_grad, 4)
+    rowz[2, z] = last_y.total()
     last_z.start()
     teacher_grad(0)
-    last_now[...] = last_z.total()
-    row_total, mixed_total, student_total = last_now[0:8], last_now[8:16], last_now[16:24]
-    row_now[...] = jnp.log(student_total) - mixed_total / row_total
-    loss_ref[...] = row_now[pl.ds(y, 1), :]
-    last_now[0:8] = 1.0 / row_total
-    last_now[16:24] = 1.0 / student_total
-    down_ref[0] = down(last_now[pl.ds(y, 1), :])
-    down_ref[1] = down(last_now[pl.ds(16 + y, 1), :])
+    each(0, NY, mixed_rows, 8)
+    mixed_y.start()
+    last_now[8:16] = student_z.total()
+    last_now[0:8] = last_z.total()
+    last_now[16:24] = 1.0 / last_now[0:8]
+    last_now[24:32] = 1.0 / last_now[8:16]
+    down_ref[0] = down(last_now[pl.ds(16 + y, 1), :])
+    down_ref[1] = down(last_now[pl.ds(24 + y, 1), :])
 
     def grad_block(d):
         b = ring(y + d, NY)
         scale = col_now[:, :B]
-        row_scale, student_scale = down(last_now[pl.ds(b, 1), :]), down(last_now[pl.ds(16 + b, 1), :])
+        row_scale, student_scale = down(last_now[pl.ds(16 + b, 1), :]), down(last_now[pl.ds(24 + b, 1), :])
         for k in range(NP):
             target = e_ref[crop_rows(d), lane_tile(k)] * scale[k : k + 1, :] * row_scale
             g_ref[crop_rows(d), lane_tile(k)] = (
                 x_ref[crop_rows(d), lane_tile(k)] * student_scale - target
             ).astype(BF16)
 
-    each(0, NY, grad_block)
+    each(0, NY, grad_block, 8)
 
     def proto_grad(half):
         def pair(n):
@@ -460,6 +503,10 @@
 
     proto_grad(1 - core)
     v_sib.start()
+    t_reduce.near_sums()
+    t_reduce.far_sums()
+    rowz[4, z] = mixed_y.total()
+    mixed_z.start()
     proto_grad(core)
 
     v_sib.recv()
@@ -467,26 +514,26 @@
     def add_sibling(i):
         v_ref[core * NX + i] += vsib[i]
 
-    each(0, NX, add_sibling)
+    each(0, NX, add_sibling, 4)
     v_x.start()
-    t_reduce.near_sums()
-    t_reduce.far_sums()
+    student_part = s_reduce.result() * down_ref[1, rows(z), 0:1]
+    teacher_part = t_reduce.result() * down_ref[0, rows(z), 0:1]
+    unit_grad = (student_part - teacher_part) * (STUDENT / CROPS)
+    gfb[rows(z)] = project(su_ref[rows(z)], unit_grad, sinv_ref[rows(z), 0:1])
+
+    def all_copy(j, source, target):
+        part = gfb.at[rows(source)]
+        return copy(part, part, gs.at[j], gr.at[j], at_z(target))
+
+    every = over_z(all_copy)
+    every.start()
+    row_now[...] = jnp.log(last_now[8:16]) - mixed_z.total() * last_now[16:24]
+    loss_ref[...] = row_now[pl.ds(y, 1), :]
 
     v_x.recv()
     vx[x] = v_ref[own]
     proto_sum = (vx[0] + vx[1] + vx[2] + vx[3]).T * (STUDENT / CROPS)
     gp_ref[...] = project(pu_ref[...], proto_sum, pinv_ref[:, 0:1])
-    student_part = s_reduce.result() * down_ref[1, rows(z), 0:1]
-    teacher_part = t_reduce.result() * down_ref[0, rows(z), 0:1]
-    unit_grad = (student_part - teacher_part) * (STUDENT / CROPS)
-    gfb[rows(z)] = project(su_ref[rows(z)], unit_grad, sinv_ref[rows(z), 0:1])
-
-    def all_copy(j, source, target):
-        part = gfb.at[rows(source)]
-        return copy(part, part, gs.at[j], gr.at[j], at_z(target))
-
-    every = over_z(all_copy)
-    every.start()
     every.recv()
     gf_ref[...] = gfb[...]
 
@@ -534,13 +581,11 @@
             pltpu.VMEM((B, 128), F32),
             pltpu.VMEM((B, 128), F32),
             pltpu.VMEM((3, 8, 8, 128), F32),
-            pltpu.VMEM((2, 8, 8, 128), F32),
-            pltpu.VMEM((2, 8, 8, 128), F32),
-            pltpu.VMEM((8, 24, 128), F32),
-            pltpu.VMEM((8, 24, 128), F32),
+            pltpu.VMEM((5, 8, 8, 128), F32),
+            pltpu.VMEM((5, 8, 8, 128), F32),
             pltpu.VMEM((8, C), F32),
             pltpu.VMEM((8, 128), F32),
-            pltpu.VMEM((24, 128), F32),
+            pltpu.VMEM((32, 128), F32),
             pltpu.VMEM((2, B, 128), F32),
             *reduce_shapes(),
             *reduce_shapes(),
@@ -549,22 +594,22 @@
             pltpu.VMEM((NX, K, B), F32),
             pltpu.VMEM((NX, K, B), F32),
             dma((3,)),
-            dma((16,)), dma((16,)),
+            dma((20,)), dma((20,)),
             dma((16,)), dma((16,)),
             dma((8,)), dma((8,)),
             dma((3, 8)), dma((3, 8)),
-            dma((3, 8)), dma((3, 8)),
-            dma((3, 8)), dma((3, 8)),
+            dma((5, 8)), dma((5, 8)),
+            dma((5, 8)), dma((5, 8)),
             dma((24,)), dma((24,)),
             dma((24,)), dma((24,)),
             dma((8,)), dma((8,)),
             dma((4,)), dma((4,)),
         ],
         compiler_params=pltpu.CompilerParams(
-            collective_id=0, has_side_effects=True, vmem_limit_bytes=60 * 1024 * 1024
+            collective_id=0, has_side_effects=True, vmem_limit_bytes=50 * 1024 * 1024
         ),
         name="dino_head",
-    )(student_features, teacher_features, prototypes)
+    )(*(pltpu.with_memory_space_constraint(a, pltpu.MemorySpace.HBM) for a in (student_features, teacher_features, prototypes)))
     return grad_features, grad_prototypes, losses.reshape(B)
 
 

time: 109 us -> 96.7 us (0.89)
  Pallas kernels: 105 us -> 94.1 us
    pallas_call x1, Pallas kernels: 105 us -> 94.1 us  [shards(): pl.pallas_call(kernel, out_shape=(jax.ShapeDtypeStruct((B, K), F32), jax....]
    unnamed x7 -> x3, local copies, waits for them, and re-layouts: 2.85 us -> 1.87 us
where the time goes in v4:
time: 96.7 us; the launch traced here: 96.6 us
  Pallas kernels  94.1 us (97%)
  local copies, waits for them, and re-layouts  1.87 us (2%)
    pallas_call x1, Pallas kernels, shards(): pl.pallas_call(kernel, out_shape=(jax.ShapeDtypeStruct((B, K), F32), jax....  94.1 us

profile of v4, /device:TPU:1, one launch (start us, length us, event | category | flops | bytes accessed | tf_op | source)
XLA Modules:
  0.0 96.6 jit_solution(13522418643108620627)
XLA Ops:
  0.6 94.1 %dino_head.1 = (f32[128,384]{1,0:T(8,128)S(1)}, f32[128,384]{1,0:T(8,128)S(1)}, f32[1,128]{1,0:T(1,128)S(1)}) custom-call(bf16[128,384]{1,0:T(8,128)(2,1)} %s_hbm.1, bf16[128,384]{1,0:T(8,128)(2,1)} %t_hbm.1, bf16[128,384]{1,0:T(8,128)(2,1)} %p_hbm.1), custom_call_target="tpu_custom_call" | custom-call | tf_op jit(solution)/shard_map/dino_head/pallas_call | solution.py:560
  94.7 0.7 copy.9
  95.4 0.7 copy.10
  96.1 0.5 copy.11

commit v5 on v4

--- a/solution.py
+++ b/solution.py
@@ -208,12 +208,14 @@
             now.recv_one(i)
             later.out(i).start()
         if later is t_steps[1]:
+            s_far.start()
             t_piece.recv()
             t_pass.start()
-    s_far.start()
     p_x.recv()
     p_passed.start()
     p_own.recv()
+    s_far.recv()
+    s_pass.start()
     s_near.start()
     p_passed.recv()
 
@@ -237,8 +239,6 @@
     for d in (3, 5):
         teacher_block(d)
     t_pass.recv()
-    s_far.recv()
-    s_pass.start()
     teacher_block(4)
 
     class Swap(Copies):
@@ -406,13 +406,14 @@
         rowz[it, z] = y_swap[it].total()
         z_swap[it].start()
         if it == 0:
+            s_reduce.near.start()
+        if it == 0:
             s_pass.recv()
             each(3, 6, student_block, 3)
         row_now[...] = 1.0 / z_swap[it].total()
         if it == 0:
             student_y.start()
             s_reduce.far.start()
-            s_reduce.near.start()
         else:
             rowz[3, z] = student_y.total()
             student_z.start()

time: 96.7 us -> 93.5 us (0.967)
  Pallas kernels: 94.1 us -> 90.8 us
    pallas_call x1, Pallas kernels: 94.1 us -> 90.8 us  [shards(): pl.pallas_call(kernel, out_shape=(jax.ShapeDtypeStruct((B, K), F32), jax....]
where the time goes in v5:
time: 93.5 us; the launch traced here: 93.3 us
  Pallas kernels  90.8 us (97%)
  local copies, waits for them, and re-layouts  1.87 us (2%)
    pallas_call x1, Pallas kernels, shards(): pl.pallas_call(kernel, out_shape=(jax.ShapeDtypeStruct((B, K), F32), jax....  90.8 us

profile of v5, /device:TPU:1, one launch (start us, length us, event | category | flops | bytes accessed | tf_op | source)
XLA Modules:
  0.0 93.3 jit_solution(12906250896463465484)
XLA Ops:
  0.6 90.8 %dino_head.1 = (f32[128,384]{1,0:T(8,128)S(1)}, f32[128,384]{1,0:T(8,128)S(1)}, f32[1,128]{1,0:T(1,128)S(1)}) custom-call(bf16[128,384]{1,0:T(8,128)(2,1)} %s_hbm.1, bf16[128,384]{1,0:T(8,128)(2,1)} %t_hbm.1, bf16[128,384]{1,0:T(8,128)(2,1)} %p_hbm.1), custom_call_target="tpu_custom_call" | custom-call | tf_op jit(solution)/shard_map/dino_head/pallas_call | solution.py:561
  91.5 0.7 copy.9
  92.2 0.7 copy.10
  92.8 0.5 copy.11

commit v6 on v5

--- a/solution.py
+++ b/solution.py
@@ -39,8 +39,8 @@
     s_ref, t_ref, p_ref,
     t_all, s_all, s_turned, p_all, e_ref, l_ref, x_ref, g_ref, su_ref, pu_ref, sinv_ref, pinv_ref,
     colx, rowy, rowz, col_now, row_now, last_now,
-    down_ref, us_ref, us_own, s_near_in, s_zfar, s_w, s_yfar, s_b, s_zn,
-    ut_ref, ut_own, t_near_in, t_zfar, t_w, t_yfar, t_b, t_zn, gfb, v_ref, vsib, vx,
+    down_ref, us_ref, us_own, s_near_in, s_zfar, s_w, s_yfar, s_b, s_b16, s_zn,
+    ut_ref, ut_own, t_near_in, t_zfar, t_w, t_yfar, t_b, t_b16, t_zn, gfb, v_ref, vsib, v_out, vx,
     ins, ts, tr, ss, sr, ps, pr, xs, xr, ys, yr, zs, zr, uss, usr, uts, utr, gs, gr, vs, vr,
 ):
     dp, z = lax.axis_index("dp"), lax.axis_index("proto")
@@ -290,8 +290,9 @@
         return jnp.dot(g_ref[crop_rows(d), :], p_all[...].reshape(C, K), preferred_element_type=F32)
 
     class Reduce:
-        def __init__(self, u, u_own, near, zfar, w, yfar, b, zn, send, recv):
+        def __init__(self, u, u_own, near, zfar, w, yfar, b, b16, zn, send, recv):
             self.bufs = u, u_own, near, zfar, w, yfar, b, zn
+            self.b16 = b16
 
             def far_copy(j, source, target):
                 part = u.at[pl.ds(3, 3), rows(target)]
@@ -306,7 +307,7 @@
                 return copy(w.at[k], yfar.at[k], send.at[12 + k], recv.at[12 + k], to)
 
             def piece_copy(j, source, target):
-                return copy(b.at[rows(target)], zn.at[source], send.at[16 + j], recv.at[16 + j], at_z(target))
+                return copy(b16.at[rows(target)], zn.at[source], send.at[16 + j], recv.at[16 + j], at_z(target))
 
             self.far, self.piece = over_z(far_copy), over_z(piece_copy)
             self.near, self.sum = Copies(0, 4, near_copy, near_copy), Copies(0, 3, sum_copy, sum_copy)
@@ -325,27 +326,28 @@
             total = zfar[0].astype(F32)
             for i in range(1, NZ):
                 total = total + zfar[i].astype(F32)
-            w[...] = total
+            w[...] = total.astype(BF16)
             self.sum.start()
 
         def near_sums(self):
             _, u_own, near, _, _, _, b, _ = self.bufs
             self.near.recv()
             b[...] = u_own[...] + sum(near[i].astype(F32) for i in range(4))
+            self.b16[...] = b[...].astype(BF16)
             self.piece.start()
 
         def result(self):
             _, _, _, _, _, yfar, b, zn = self.bufs
             self.piece.recv()
             self.sum.recv()
-            zn[z] = b[rows(z)]
-            total = yfar[0] + yfar[1] + yfar[2]
+            zn[z] = jnp.zeros((PIECE, K), BF16)
+            total = b[rows(z)] + sum(yfar[i].astype(F32) for i in range(3))
             for i in range(NZ):
-                total = total + zn[i]
+                total = total + zn[i].astype(F32)
             return total
 
-    s_reduce = Reduce(us_ref, us_own, s_near_in, s_zfar, s_w, s_yfar, s_b, s_zn, uss, usr)
-    t_reduce = Reduce(ut_ref, ut_own, t_near_in, t_zfar, t_w, t_yfar, t_b, t_zn, uts, utr)
+    s_reduce = Reduce(us_ref, us_own, s_near_in, s_zfar, s_w, s_yfar, s_b, s_b16, s_zn, uss, usr)
+    t_reduce = Reduce(ut_ref, ut_own, t_near_in, t_zfar, t_w, t_yfar, t_b, t_b16, t_zn, uts, utr)
 
     def student_block(d):
         block = s_all[d]
@@ -438,9 +440,6 @@
             mixed = mixed + scaled * l_ref[crop_rows(d), lane_tile(k)]
         rowy[4, y, pl.ds(ring(y + d, NY), 1), :] = lane_rows(mixed)
 
-    each(0, NY, last_rows, 8)
-    last_y.start()
-
     def teacher_grad(d):
         scale = col_now[:, :B]
         for k in range(NP):
@@ -450,6 +449,8 @@
         t_reduce.put(d, times_protos(d))
 
     each(3, 6, teacher_grad, 3)
+    each(0, NY, last_rows, 8)
+    last_y.start()
     t_reduce.far.start()
 
     def near_grad(i):
@@ -465,6 +466,8 @@
     mixed_y.start()
     last_now[8:16] = student_z.total()
     last_now[0:8] = last_z.total()
+    t_reduce.near_sums()
+    t_reduce.far_sums()
     last_now[16:24] = 1.0 / last_now[0:8]
     last_now[24:32] = 1.0 / last_now[8:16]
     down_ref[0] = down(last_now[pl.ds(16 + y, 1), :])
@@ -495,17 +498,13 @@
         return copy(v_ref.at[pl.ds(who * NX, NX)], vsib, vs.at[0], vr.at[0], at_p((1 - core) * NX + x))
 
     def v_x_copy(j, source, target):
-        return copy(
-            v_ref.at[core * NX + target], vx.at[source], vs.at[j], vr.at[j], at_p(core * NX + target)
-        )
+        return copy(v_out.at[target], vx.at[source], vs.at[j], vr.at[j], at_p(core * NX + target))
 
     v_sib = Copies(0, 1, lambda i: v_sib_copy(1 - core), lambda i: v_sib_copy(1 - core))
     v_x = over_x(v_x_copy)
 
     proto_grad(1 - core)
     v_sib.start()
-    t_reduce.near_sums()
-    t_reduce.far_sums()
     rowz[4, z] = mixed_y.total()
     mixed_z.start()
     proto_grad(core)
@@ -513,7 +512,9 @@
     v_sib.recv()
 
     def add_sibling(i):
-        v_ref[core * NX + i] += vsib[i]
+        total = v_ref[core * NX + i] + vsib[i]
+        v_ref[core * NX + i] = total
+        v_out[i] = total.astype(BF16)
 
     each(0, NX, add_sibling, 4)
     v_x.start()
@@ -532,8 +533,8 @@
     loss_ref[...] = row_now[pl.ds(y, 1), :]
 
     v_x.recv()
-    vx[x] = v_ref[own]
-    proto_sum = (vx[0] + vx[1] + vx[2] + vx[3]).T * (STUDENT / CROPS)
+    vx[x] = jnp.zeros((K, B), BF16)
+    proto_sum = (v_ref[own] + sum(vx[i].astype(F32) for i in range(NX))).T * (STUDENT / CROPS)
     gp_ref[...] = project(pu_ref[...], proto_sum, pinv_ref[:, 0:1])
     every.recv()
     gf_ref[...] = gfb[...]
@@ -548,10 +549,11 @@
         pltpu.VMEM((B, K), F32),
         pltpu.VMEM((4, B, K), BF16),
         pltpu.VMEM((NZ, 3, PIECE, K), BF16),
-        pltpu.VMEM((3, PIECE, K), F32),
-        pltpu.VMEM((3, PIECE, K), F32),
+        pltpu.VMEM((3, PIECE, K), BF16),
+        pltpu.VMEM((3, PIECE, K), BF16),
         pltpu.VMEM((B, K), F32),
-        pltpu.VMEM((NZ, PIECE, K), F32),
+        pltpu.VMEM((B, K), BF16),
+        pltpu.VMEM((NZ, PIECE, K), BF16),
     ]
 
 
@@ -593,7 +595,8 @@
             pltpu.VMEM((B, K), F32),
             pltpu.VMEM((NP, K, B), F32),
             pltpu.VMEM((NX, K, B), F32),
-            pltpu.VMEM((NX, K, B), F32),
+            pltpu.VMEM((NX, K, B), BF16),
+            pltpu.VMEM((NX, K, B), BF16),
             dma((3,)),
             dma((20,)), dma((20,)),
             dma((16,)), dma((16,)),

time: 93.5 us -> 89.8 us (0.960)
  Pallas kernels: 90.8 us -> 87.1 us
    pallas_call x1, Pallas kernels: 90.8 us -> 87.1 us  [shards(): pl.pallas_call(kernel, out_shape=(jax.ShapeDtypeStruct((B, K), F32), jax....]
where the time goes in v6:
time: 89.8 us; the launch traced here: 89.6 us
  Pallas kernels  87.1 us (97%)
  local copies, waits for them, and re-layouts  1.87 us (2%)
    pallas_call x1, Pallas kernels, shards(): pl.pallas_call(kernel, out_shape=(jax.ShapeDtypeStruct((B, K), F32), jax....  87.1 us
    unnamed x3, local copies, waits for them, and re-layouts  1.87 us

profile of v6, /device:TPU:1, one launch (start us, length us, event | category | flops | bytes accessed | tf_op | source)
XLA Modules:
  0.0 89.6 jit_solution(4480979103803714603)
XLA Ops:
  0.6 87.1 %dino_head.1 = (f32[128,384]{1,0:T(8,128)S(1)}, f32[128,384]{1,0:T(8,128)S(1)}, f32[1,128]{1,0:T(1,128)S(1)}) custom-call(bf16[128,384]{1,0:T(8,128)(2,1)} %s_hbm.1, bf16[128,384]{1,0:T(8,128)(2,1)} %t_hbm.1, bf16[128,384]{1,0:T(8,128)(2,1)} %p_hbm.1), custom_call_target="tpu_custom_call" | custom-call | tf_op jit(solution)/shard_map/dino_head/pallas_call | solution.py:563
  87.7 0.7 copy.9
  88.4 0.7 copy.10
  89.1 0.5 copy.11

commit v7 on v6

--- a/solution.py
+++ b/solution.py
@@ -40,7 +40,7 @@
     t_all, s_all, s_turned, p_all, e_ref, l_ref, x_ref, g_ref, su_ref, pu_ref, sinv_ref, pinv_ref,
     colx, rowy, rowz, col_now, row_now, last_now,
     down_ref, us_ref, us_own, s_near_in, s_zfar, s_w, s_yfar, s_b, s_b16, s_zn,
-    ut_ref, ut_own, t_near_in, t_zfar, t_w, t_yfar, t_b, t_b16, t_zn, gfb, v_ref, vsib, v_out, vx,
+    ut_ref, ut_own, t_near_in, t_zfar, t_w, t_yfar, t_b, t_b16, t_zn, gfb, v_ref, vsib, v_out, v_opposite_in, vx,
     ins, ts, tr, ss, sr, ps, pr, xs, xr, ys, yr, zs, zr, uss, usr, uts, utr, gs, gr, vs, vr,
 ):
     dp, z = lax.axis_index("dp"), lax.axis_index("proto")
@@ -498,10 +498,21 @@
         return copy(v_ref.at[pl.ds(who * NX, NX)], vsib, vs.at[0], vr.at[0], at_p((1 - core) * NX + x))
 
     def v_x_copy(j, source, target):
-        return copy(v_out.at[target], vx.at[source], vs.at[j], vr.at[j], at_p(core * NX + target))
+        return copy(
+            v_ref.at[core * NX + target], vx.at[source], vs.at[j], vr.at[j], at_p(core * NX + target)
+        )
+
+    def v_opposite_copy(i):
+        return copy(v_out, v_opposite_in, vs.at[2], vr.at[2], at_p(core * NX + ring(x + 2, NX)))
 
     v_sib = Copies(0, 1, lambda i: v_sib_copy(1 - core), lambda i: v_sib_copy(1 - core))
-    v_x = over_x(v_x_copy)
+    v_x = Copies(
+        0,
+        2,
+        lambda i: v_x_copy(1 + 2 * i, x, ring(x + 1 + 2 * i, NX)),
+        lambda i: v_x_copy(1 + 2 * i, ring(x - 1 - 2 * i, NX), ring(x + 1 + 2 * i, NX)),
+    )
+    v_opposite = Copies(0, 1, v_opposite_copy, v_opposite_copy)
 
     proto_grad(1 - core)
     v_sib.start()
@@ -512,11 +523,11 @@
     v_sib.recv()
 
     def add_sibling(i):
-        total = v_ref[core * NX + i] + vsib[i]
-        v_ref[core * NX + i] = total
-        v_out[i] = total.astype(BF16)
+        v_ref[core * NX + i] += vsib[i]
 
     each(0, NX, add_sibling, 4)
+    v_out[...] = v_ref[core * NX + ring(x + 2, NX)].astype(BF16)
+    v_opposite.start()
     v_x.start()
     student_part = s_reduce.result() * down_ref[1, rows(z), 0:1]
     teacher_part = t_reduce.result() * down_ref[0, rows(z), 0:1]
@@ -533,8 +544,9 @@
     loss_ref[...] = row_now[pl.ds(y, 1), :]
 
     v_x.recv()
-    vx[x] = jnp.zeros((K, B), BF16)
-    proto_sum = (v_ref[own] + sum(vx[i].astype(F32) for i in range(NX))).T * (STUDENT / CROPS)
+    v_opposite.recv()
+    proto_sum = v_ref[own] + vx[ring(x + 1, NX)] + vx[ring(x - 1, NX)] + v_opposite_in[...].astype(F32)
+    proto_sum = proto_sum.T * (STUDENT / CROPS)
     gp_ref[...] = project(pu_ref[...], proto_sum, pinv_ref[:, 0:1])
     every.recv()
     gf_ref[...] = gfb[...]
@@ -595,8 +607,9 @@
             pltpu.VMEM((B, K), F32),
             pltpu.VMEM((NP, K, B), F32),
             pltpu.VMEM((NX, K, B), F32),
-            pltpu.VMEM((NX, K, B), BF16),
-            pltpu.VMEM((NX, K, B), BF16),
+            pltpu.VMEM((K, B), BF16),
+            pltpu.VMEM((K, B), BF16),
+            pltpu.VMEM((NX, K, B), F32),
             dma((3,)),
             dma((20,)), dma((20,)),
             dma((16,)), dma((16,)),

time: 89.8 us -> 91.8 us (1.022)
  Pallas kernels: 87.1 us -> 89.2 us
    pallas_call x1, Pallas kernels: 87.1 us -> 89.2 us  [shards(): pl.pallas_call(kernel, out_shape=(jax.ShapeDtypeStruct((B, K), F32), jax....]
where the time goes in v7:
time: 91.8 us; the launch traced here: 91.7 us
  Pallas kernels  89.2 us (97%)
  local copies, waits for them, and re-layouts  1.87 us (2%)
    pallas_call x1, Pallas kernels, shards(): pl.pallas_call(kernel, out_shape=(jax.ShapeDtypeStruct((B, K), F32), jax....  89.2 us
    unnamed x3, local copies, waits for them, and re-layouts  1.87 us

profile of v7, /device:TPU:1, one launch (start us, length us, event | category | flops | bytes accessed | tf_op | source)
XLA Modules:
  0.0 91.7 jit_solution(157745400554738026)
XLA Ops:
  0.6 89.2 %dino_head.1 = (f32[128,384]{1,0:T(8,128)S(1)}, f32[128,384]{1,0:T(8,128)S(1)}, f32[1,128]{1,0:T(1,128)S(1)}) custom-call(bf16[128,384]{1,0:T(8,128)(2,1)} %s_hbm.1, bf16[128,384]{1,0:T(8,128)(2,1)} %t_hbm.1, bf16[128,384]{1,0:T(8,128)(2,1)} %p_hbm.1), custom_call_target="tpu_custom_call" | custom-call | tf_op jit(solution)/shard_map/dino_head/pallas_call | solution.py:575
  89.8 0.7 copy.9
  90.5 0.7 copy.10
  91.2 0.5 copy.11
